TPU v7x, 128 devices: a whole 4x4x4 slice. The times are simulated.
128 devices in a mesh: lon: 16 (over x, z), lat: 8 (over y, core).
Axes of the slice: x: 4, y: 4, z: 4, core: 2. Of those that a mesh axis runs over, the one named last changes fastest.
Arguments:
- ocean_state: float32 [4, 20, 1024, 4096], P(None, None, 'lat', 'lon'), may hold values from -6 to 6
- canopy_type: int32 [1024, 4096], P('lat', 'lon'), may hold values from 0 to 7
- drag_table: float32 [8, 20], replicated, may hold values from 0.1 to 10
- ocean_list: int32 [128, 16384], P(('lon', 'lat')), may hold values from -1 to 32767, as said below
- ice_list: int32 [128, 16384], P(('lon', 'lat')), may hold values from -1 to 8191, as said below
- weight_list: int32 [128, 16384], P(('lon', 'lat')), may hold values from -1 to 63, as said below
- area_table: float32 [64], replicated, may hold values from 0.05 to 1
- ice_temp: float32 [128, 8192], P(('lon', 'lat')), may hold values from -6 to 6
- ice_cond: float32 [128, 8192], P(('lon', 'lat')), may hold values from 0.3 to 3
- ice_vel: float32 [128, 2, 8192], P(('lon', 'lat')), may hold values from -6 to 6
Outputs:
- ocean_next: float32 [4, 20, 1024, 4096], P(None, None, 'lat', 'lon')
- ice_temp_next: float32 [128, 8192], P(('lon', 'lat'))
Inputs may be any that keep to these rules, and one draw needn't show every extreme that they name: `ocean_list`: entry [s, d * 128 + c] is the surface cell (row * 256 + column within source s's block) of slot c of the pair (s, d); used slots come first in each pair, the rest hold -1. A pair uses at most 128 slots, and some device receives 128 from every source. `ice_list`: entry [d, s * 128 + c] is the ice cell on device d of the same slot of the pair (s, d); -1 exactly where ocean_list is -1. `weight_list`: entry [d, s * 128 + c] is the area weight index of the same slot; -1 exactly where ocean_list is -1.
All inputs are finite; a program needn't handle non-finite values.
Results may differ from a plain program's by a relative error of at most 0.0001.
Values sent between devices are 32-bit elements; how exact they have to be, the bound alone decides.
A program may use at most 192 MiB of HBM per device.

v0:
```python
import math

import jax
import jax.numpy as jnp
from jax import lax
from jax.sharding import PartitionSpec as P

TIME_STEP = 0.1
FLUX_STEP = 0.5
DIFFUSIVITY = 0.1
VISCOSITY = 0.1
THERMAL_EXP = 0.2
HALINE_CONTRACT = 0.8
GRAV_LAYER = 0.5
CORIOLIS = 1.0
VERTICAL_MIX = 0.5
ICE_RATE = 0.25
ICE_DRAG = 0.5
BRINE_RATE = 0.5
SPEED_BACKGROUND = 0.01
FOLD_SIGNS = (1.0, 1.0, -1.0, -1.0)


def extended_2(array, sides, width, wrap):
    for axis, dim in sides:
        size, length = (lax.axis_size(axis), array.shape[dim])
        up = [(i, (i + 1) % size) for i in range(size if wrap else size - 1)]
        down = [(j, i) for i, j in up]
        last = lax.slice_in_dim(array, length - width, length, axis=dim)
        initial = lax.slice_in_dim(array, 0, width, axis=dim)
        before = lax.ppermute(last, axis, up)
        after = lax.ppermute(initial, axis, down)
        array = jnp.concatenate([before, array, after], axis=dim)
    return array


def partner(block, axis, apart):
    count = lax.axis_size(axis)
    route = []
    for low in range(count):
        high = low | 1 << apart
        if high != low and high < count:
            route += [(low, high), (high, low)]
    return lax.ppermute(block, axis, route)


def neighbours(values):
    return (
        values[..., 1:-1, 1:-1],
        values[..., 1:-1, 2:],
        values[..., 1:-1, :-2],
        values[..., 2:, 1:-1],
        values[..., :-2, 1:-1],
    )


def provisional(extended, coriolis):
    centre, east_side, west_side, north_side, south_side = neighbours(extended)
    density = HALINE_CONTRACT * extended[1] - THERMAL_EXP * extended[0]
    above_sum = jnp.cumsum(density, axis=0) - density
    pressure = GRAV_LAYER * (above_sum + 0.5 * density)
    pressure_sides = neighbours(pressure)
    face_east = 0.5 * (centre[2] + east_side[2])
    face_west = 0.5 * (west_side[2] + centre[2])
    face_north = 0.5 * (centre[3] + north_side[3])
    face_south = 0.5 * (south_side[3] + centre[3])
    advection = (
        face_east * 0.5 * (centre + east_side)
        - face_west * 0.5 * (west_side + centre)
        + face_north * 0.5 * (centre + north_side)
        - face_south * 0.5 * (south_side + centre)
    )
    laplace = east_side + west_side + north_side + south_side - 4.0 * centre
    tracers = centre[0:2] + TIME_STEP * (DIFFUSIVITY * laplace[0:2] - advection[0:2])
    u_next = centre[2] + TIME_STEP * (
        coriolis * centre[3]
        - 0.5 * (pressure_sides[1] - pressure_sides[2])
        + VISCOSITY * laplace[2]
        - advection[2]
    )
    v_next = centre[3] + TIME_STEP * (
        -coriolis * centre[2]
        - 0.5 * (pressure_sides[3] - pressure_sides[4])
        + VISCOSITY * laplace[3]
        - advection[3]
    )
    return jnp.concatenate([tracers, u_next[None], v_next[None]], axis=0)


def vertical_mix(column_data):
    depth = column_data.shape[1]
    upper_terms = []
    right_terms = []
    divisor = 1.0 + VERTICAL_MIX
    upper = -VERTICAL_MIX / divisor
    right_side = column_data[:, 0] / divisor
    upper_terms.append(upper)
    right_terms.append(right_side)
    for depth_index in range(1, depth):
        diagonal = 1.0 + VERTICAL_MIX if depth_index == depth - 1 else 1.0 + 2.0 * VERTICAL_MIX
        divisor = diagonal + VERTICAL_MIX * upper
        upper = -VERTICAL_MIX / divisor
        right_side = (column_data[:, depth_index] + VERTICAL_MIX * right_side) / divisor
        upper_terms.append(upper)
        right_terms.append(right_side)
    solved = [right_terms[-1]]
    for depth_index in range(depth - 2, -1, -1):
        solved.append(right_terms[depth_index] - upper_terms[depth_index] * solved[-1])
    return jnp.stack(solved[::-1], axis=1)


def finish(provisional_state, surface_flux, drag_coef):
    forced = provisional_state.at[:, 0].add(FLUX_STEP * surface_flux)
    drift_speed = jnp.sqrt(forced[2] * forced[2] + forced[3] * forced[3] + SPEED_BACKGROUND)
    damping = 1.0 / (1.0 + TIME_STEP * drag_coef * drift_speed)
    damped = jnp.concatenate([forced[0:2], forced[2:4] * damping[None]], axis=0)
    return vertical_mix(damped)


def slot_fluxes(arrived, area_weight, temp_ice, cond_ice, u_ice, v_ice):
    drift_u = u_ice - arrived[2]
    drift_v = v_ice - arrived[3]
    drift_speed = jnp.sqrt(drift_u * drift_u + drift_v * drift_v + SPEED_BACKGROUND)
    heat_flux = area_weight * cond_ice * (temp_ice - arrived[0])
    salt_flux = -BRINE_RATE * area_weight * cond_ice * arrived[1]
    stress_u = ICE_DRAG * area_weight * drift_speed * drift_u
    stress_v = ICE_DRAG * area_weight * drift_speed * drift_v
    return jnp.stack([heat_flux, salt_flux, stress_u, stress_v])


def one_hot_rows(index, width, in_use):
    positions = jnp.arange(width, dtype=jnp.int32)[:, None]
    return ((index[None, :] == positions) & in_use[None, :]).astype(jnp.float32)


def pick_slots(table, high_hot, low_hot):
    fields = table.shape[0]
    high_count = high_hot.shape[0]
    low_count = low_hot.shape[0]
    blocks = jnp.dot(
        table.reshape(fields * high_count, low_count),
        low_hot,
        precision=lax.Precision.HIGHEST,
        preferred_element_type=jnp.float32,
    )
    return jnp.sum(blocks.reshape(fields, high_count, -1) * high_hot[None], axis=1)


def spread_slots(values, high_hot, low_hot):
    fields = values.shape[0]
    high_count = high_hot.shape[0]
    weighted = (values[:, None, :] * high_hot[None]).reshape(fields * high_count, -1)
    summed = lax.dot_general(
        weighted,
        low_hot,
        (((1,), (1,)), ((), ())),
        precision=lax.Precision.HIGHEST,
        preferred_element_type=jnp.float32,
    )
    return summed.reshape(fields, high_count * low_hot.shape[0])


def shards(
    ocean_state,
    canopy_type,
    drag_table,
    ocean_list,
    ice_list,
    weight_list,
    area_table,
    ice_temp,
    ice_cond,
    ice_vel,
):
    components, levels, block_rows, block_cols = ocean_state.shape
    lon_count = lax.axis_size("lon")
    lat_count = lax.axis_size("lat")
    devices = lon_count * lat_count
    slot_count = ocean_list.shape[1] // devices
    lat_index = lax.axis_index("lat")
    cell_flat = ocean_list.reshape(-1)
    in_use = cell_flat >= 0
    safe_cell = jnp.where(in_use, cell_flat, 0)
    cell_row_hot = one_hot_rows(safe_cell // block_cols, block_rows, in_use)
    cell_col_hot = one_hot_rows(safe_cell % block_cols, block_cols, in_use)
    surface = ocean_state[:, 0].reshape(components, block_rows * block_cols)
    outgoing = pick_slots(surface, cell_row_hot, cell_col_hot).reshape(
        components, devices, slot_count
    )
    arrived = lax.all_to_all(outgoing, ("lon", "lat"), split_axis=1, concat_axis=1, tiled=True)
    ice_cells = ice_list.reshape(-1)
    ice_used = ice_cells >= 0
    safe_ice = jnp.where(ice_used, ice_cells, 0)
    ice_count = ice_temp.shape[1]
    ice_low = math.gcd(ice_count, 128)
    ice_high = ice_count // ice_low
    ice_high_hot = one_hot_rows(safe_ice // ice_low, ice_high, ice_used)
    ice_low_hot = one_hot_rows(safe_ice % ice_low, ice_low, ice_used)
    ice_fields = jnp.stack([ice_temp[0], ice_cond[0], ice_vel[0, 0], ice_vel[0, 1]])
    picked = pick_slots(ice_fields, ice_high_hot, ice_low_hot).reshape(4, devices, slot_count)
    weight_index = weight_list.reshape(devices, slot_count)
    table_rows = jnp.arange(area_table.shape[0])
    area_weight = jnp.sum(
        (weight_index[None] == table_rows[:, None, None]).astype(jnp.float32)
        * area_table[:, None, None],
        axis=0,
    )
    fluxes = slot_fluxes(arrived, area_weight, picked[0], picked[1], picked[2], picked[3])
    heat_sum = spread_slots(fluxes[0].reshape(1, -1), ice_high_hot, ice_low_hot)
    ice_temp_next = ice_temp - ICE_RATE * heat_sum
    returned = lax.all_to_all(fluxes, ("lon", "lat"), split_axis=1, concat_axis=1, tiled=True)
    tall_state = extended_2(ocean_state, (("lat", 2),), 1, False)
    extended = extended_2(tall_state, (("lon", 3),), 1, True)
    top_row = ocean_state[:, :, block_rows - 1, :]
    moving = top_row[:, :, ::-1]
    for bit in range(lon_count.bit_length() - 1):
        moving = partner(moving, "lon", bit)
    fold_sign = jnp.array(FOLD_SIGNS, jnp.float32)[:, None, None]
    folded = jnp.where(
        lat_index == lat_count - 1, moving * fold_sign, extended[:, :, block_rows + 1, 1:-1]
    )
    extended = extended.at[:, :, block_rows + 1, 1:-1].set(folded)
    rows_global = (lat_index * block_rows + jnp.arange(block_rows)).astype(jnp.float32)
    coriolis = (CORIOLIS * (2.0 * (rows_global + 0.5) / (block_rows * lat_count) - 1.0))[:, None]
    provisional_state = provisional(extended, coriolis)
    kind_mask = (canopy_type[None] == jnp.arange(drag_table.shape[0])[:, None, None]).astype(
        jnp.float32
    )
    drag_coef = jnp.einsum("tk,tji->kji", drag_table, kind_mask, precision=lax.Precision.HIGHEST)
    surface_flux = spread_slots(
        returned.reshape(components, -1), cell_row_hot, cell_col_hot
    ).reshape(components, block_rows, block_cols)
    ocean_next = finish(provisional_state, surface_flux, drag_coef)
    return (ocean_next, ice_temp_next)


def solution(mesh):
    return jax.shard_map(
        shards,
        mesh=mesh,
        in_specs=(
            P(None, None, "lat", "lon"),
            P("lat", "lon"),
            P(),
            P(("lon", "lat"), None),
            P(("lon", "lat"), None),
            P(("lon", "lat"), None),
            P(),
            P(("lon", "lat"), None),
            P(("lon", "lat"), None),
            P(("lon", "lat"), None, None),
        ),
        out_specs=(P(None, None, "lat", "lon"), P(("lon", "lat"), None)),
        check_vma=False,
    )
```

profile of v0, /device:TPU:1, one launch (start us, length us, event | category | flops | bytes accessed | tf_op | source)
XLA Modules:
  0.0 306.6 jit_solution(10289352757496051)
XLA Ops:
  0.7 1.5 fusion.182
  2.1 3.3 %collective-permute-start.1 = (f32[4,20,1,256]{3,2,1,0:T(1,128)S(1)}, f32[4,20,1,256]{3,2,1,0:T(1,128)S(1)}, u32[]{:S(2)}, u32[]{:S(2)}) collective-permute-start(f32[4,20,1,256]{3,2,1,0:T(1,128)S(1)} %get-tuple-element.83), channel_id=1, source_target_pairs={{1,0},{2,1},{3,2},{4,3},{5,4},{6,5},{7,6},{9,8},{10,9},{11,10},{12... | collective-permute-start | bytes 245768 | tf_op jit(solution)/shard_map/ppermute | solution.py:32
  5.5 3.2 %collective-permute-start = (f32[4,20,1,256]{3,2,1,0:T(1,128)S(1)}, f32[4,20,1,256]{3,2,1,0:T(1,128)}, u32[]{:S(2)}, u32[]{:S(2)}) collective-permute-start(f32[4,20,1,256]{3,2,1,0:T(1,128)S(1)} %get-tuple-element.82), channel_id=1, source_target_pairs={{0,1},{1,2},{2,3},{3,4},{4,5},{5,6},{6,7},{8,9},{9,10},{10,11},{11... | collective-permute-start | bytes 245768 | tf_op jit(solution)/shard_map/ppermute | solution.py:31
  8.7 0.9 rev.3
  9.6 1.6 collective-permute-start.4
  11.2 1.2 and_select_fusion
  12.4 1.0 compare_reduce_fusion
  13.5 1.2 fusion.17
  14.8 16.6 %multiply_reduce_fusion = f32[4,16384]{1,0:T(4,128)} fusion(f32[128,16384]{1,0:T(8,128)S(1)} %fusion.17, f32[512,256]{1,0:T(8,128)S(1)} %bitcast.156, s32[16384]{0:T(1024)S(1)} %bitcast.179, pred[16384]{0:T(1024)(128)(4,1)S(1)} %compare_reduce_fusion), kind=kOutput, calls=%fused_computation.40 | convolution fusion | flops 25794904064 | bytes 9256960 | tf_op jit(solution)/shard_map/dot_general | solution.py:140
  31.4 9.8 %all-to-all-start = ((f32[4,128,128]{2,0,1:T(4,128)}), f32[4,128,128]{2,0,1:T(4,128)S(1)}, u32[]{:S(2)}, u32[]{:S(2)}) async-start(f32[4,128,128]{2,0,1:T(4,128)} %bitcast.33), calls=%async_computation | async-start | bytes 524288 | tf_op jit(solution)/shard_map/all_to_all | solution.py:190
  42.7 2.7 fusion.196
  45.4 9.8 %fusion.32 = f32[4,16384]{1,0:T(4,128)S(1)} fusion(f32[64,16384]{1,0:T(8,128)S(1)} %fusion.27, s32[16384]{0:T(1024)S(1)} %bitcast.158, pred[16384]{0:T(1024)(128)(4,1)S(1)} %compare_reduce_fusion.1, f32[1,64,128]{2,1,0:T(8,128)S(1)} %bitcast.177, f32[1,64,128]{2,1,0:T(8,128)S(1)} %bitcast.176, f32[1,64,128]{2,1,0:T(8,128)S(1)} %bitcast.181, ...), kind=kOutput, calls=%fused_computation.84 | convolution fusion | flops 6455066624 | bytes 4669440 | tf_op jit(solution)/shard_map/dot_general | solution.py:140
  55.2 0.9 fusion.184
  56.1 3.1 %fusion.85 = f32[128,256,20]{1,2,0:T(8,128)} fusion(s32[128,256]{1,0:T(8,128)S(1)} %copy-done.18, f32[8,20]{1,0:T(8,128)S(1)} %copy-done), kind=kOutput, calls=%fused_computation.139 | convolution fusion | flops 63176704 | bytes 2753152 | tf_op jit(solution)/shard_map/tk,tji->kji/dot_general | solution.py:229
  59.2 1.1 select_reduce_fusion
  60.3 5.3 %pad_maximum_fusion.1 = f32[4,20,130,256]{3,2,1,0:T(8,128)S(1)} fusion(f32[4,20,1,256]{3,2,1,0:T(1,128)S(1)} %collective-permute-done.1, f32[4,20,128,256]{3,2,1,0:T(8,128)} %param.15, f32[4,20,1,256]{3,2,1,0:T(1,128)} %collective-permute-done), kind=kLoop, calls=%fused_computation.49 | loop fusion | flops 5324800 | bytes 21299200 | tf_op jit(solution)/shard_map/concatenate | solution.py:33
  65.6 6.1 %fusion.180 = (f32[4,20,130,1]{3,2,1,0:T(8,128)}, f32[4,20,130,1]{3,2,1,0:T(8,128)}) fusion(f32[4,20,130,256]{3,2,1,0:T(8,128)S(1)} %pad_maximum_fusion.1), kind=kLoop, calls=%fused_computation.264 | loop fusion | bytes 166400 | tf_op jit(solution)/shard_map/slice | solution.py:29
  71.7 4.8 %copy.56 = f32[4,20,130,1]{2,0,3,1:T(4,128)S(1)} copy(f32[4,20,130,1]{3,2,1,0:T(8,128)} %get-tuple-element.79) | data formatting | bytes 83200 | tf_op jit(solution)/shard_map/slice | solution.py:30
  76.5 5.7 %collective-permute-start.3 = (f32[4,20,130,1]{2,0,3,1:T(4,128)S(1)}, f32[4,20,130,1]{2,0,3,1:T(4,128)S(1)}, u32[]{:S(2)}, u32[]{:S(2)}) collective-permute-start(f32[4,20,130,1]{2,0,3,1:T(4,128)S(1)} %copy.56), channel_id=1, source_target_pairs={{8,0},{16,8},{24,16},{32,24},{40,32},{48,40},{56,48},{64,56},{72,6... | collective-permute-start | bytes 124808 | tf_op jit(solution)/shard_map/ppermute | solution.py:32
  82.2 4.8 %copy.55 = f32[4,20,130,1]{2,0,3,1:T(4,128)S(1)} copy(f32[4,20,130,1]{3,2,1,0:T(8,128)} %get-tuple-element.78) | data formatting | bytes 83200 | tf_op jit(solution)/shard_map/slice | solution.py:29
  87.2 3.4 %copy.58 = f32[4,20,130,1]{3,2,1,0:T(8,128)} copy(f32[4,20,130,1]{2,0,3,1:T(4,128)S(1)} %collective-permute-done.3) | data formatting | bytes 83200 | tf_op jit(solution)/shard_map/ppermute | solution.py:32
  90.6 3.5 %collective-permute-done.2 = f32[4,20,130,1]{2,0,3,1:T(4,128)S(1)} collective-permute-done((f32[4,20,130,1]{2,0,3,1:T(4,128)S(1)}, f32[4,20,130,1]{2,0,3,1:T(4,128)S(1)}, u32[]{:S(2)}, u32[]{:S(2)}) %collective-permute-start.2) | collective-permute-done | bytes 41632 | tf_op jit(solution)/shard_map/ppermute | solution.py:31
  94.1 3.4 %copy.57 = f32[4,20,130,1]{3,2,1,0:T(8,128)} copy(f32[4,20,130,1]{2,0,3,1:T(4,128)S(1)} %collective-permute-done.2) | data formatting | bytes 83200 | tf_op jit(solution)/shard_map/ppermute | solution.py:31
  97.7 17.8 %pad_maximum_fusion = f32[4,20,130,258]{3,2,1,0:T(8,128)} fusion(f32[4,20,130,1]{3,2,1,0:T(8,128)} %copy.58, f32[4,20,1,256]{3,2,1,0:T(1,128)S(1)} %collective-permute-done.1, f32[4,20,128,256]{3,2,1,0:T(8,128)} %param.15, f32[4,20,1,256]{3,2,1,0:T(1,128)} %collective-permute-done, f32[4,20,130,1]{3,2,1,0:T(8,128)} %copy.57), kind=kLoop, calls=%fused_computation.48 | loop fusion | flops 10732800 | bytes 21465600 | tf_op jit(solution)/shard_map/concatenate | solution.py:33
  116.3 0.9 copy.68
  117.2 9.3 %all-to-all-start.1 = ((f32[4,128,128]{2,0,1:T(4,128)}), f32[4,128,128]{2,0,1:T(4,128)S(1)}, u32[]{:S(2)}, u32[]{:S(2)}) async-start(f32[4,128,128]{2,0,1:T(4,128)} %copy.68), calls=%async_computation.1 | async-start | bytes 524288 | tf_op jit(solution)/shard_map/all_to_all | solution.py:211
  126.6 5.3 %fusion.80 = f32[64,128]{1,0:T(8,128)S(1)} fusion(pred[16384]{0:T(1024)(128)(4,1)S(1)} %copy-done.11, f32[16384]{0:T(1024)S(1)} %fusion.149, s32[16384]{0:T(1024)S(1)} %bitcast.167, pred[128,16384]{1,0:T(32,128)(4,1)S(1)} %copy-done.5), kind=kOutput, calls=%fused_computation.137 | convolution fusion | flops 1613766656 | bytes 2277376 | tf_op jit(solution)/shard_map/dot_general | solution.py:153
  132.7 15.6 %scatter.4 = f32[4,20,130,258]{3,2,1,0:T(8,128)} dynamic-update-slice(f32[4,20,130,258]{3,2,1,0:T(8,128)} %pad_maximum_fusion, f32[4,20,1,256]{3,2,1,0:T(1,128)S(1)} %copy.61, s32[]{:T(128)} %constant.193.clone.1, s32[]{:T(128)} %constant.193.clone.1, s32[]{:T(128)} %constant.194.clone.1, s32[]{:T(128)} %constant.195.clone.1) | dynamic-update-slice | bytes 163844 | tf_op jit(solution)/shard_map/scatter | solution.py:222
  148.3 12.3 %fusion.65 = (f32[20,128,256]{2,1,0:T(8,128)S(1)}, f32[20,128,256]{2,1,0:T(8,128)}, f32[20,128,256]{2,1,0:T(8,128)}, f32[20,128,256]{2,1,0:T(8,128)}) fusion(f32[4,20,130,258]{3,2,1,0:T(8,128)} %scatter.4), kind=kLoop, calls=%fused_computation.127 | loop fusion | flops 5242880 | bytes 26214400 | tf_op jit(solution)/shard_map/mul | solution.py:68
  160.6 9.3 %add_multiply_fusion = f32[20,130,258]{2,1,0:T(8,128)} fusion(f32[4,20,130,258]{3,2,1,0:T(8,128)} %scatter.4), kind=kOutput, calls=%fused_computation.83 | output fusion | flops 19453200 | bytes 13416000 | tf_op jit(solution)/shard_map/jit(cumsum)/reduce_window_sum | solution.py:60
  169.9 37.1 %multiply_subtract_fusion.1 = (f32[4,20,128,256]{3,2,1,0:T(8,128)}, f32[4,20,128,256]{3,2,1,0:T(8,128)}) fusion(f32[4,20,130,258]{3,2,1,0:T(8,128)} %scatter.4, f32[20,128,256]{2,1,0:T(8,128)} %get-tuple-element.77, f32[20,128,256]{2,1,0:T(8,128)} %get-tuple-element.76, f32[20,128,256]{2,1,0:T(8,128)} %get-tuple-element.75, ...), kind=kLoop, calls=%fused_computation.52 | loop fusion | flops 41943040 | bytes 83886080 | tf_op jit(solution)/shard_map/sub | solution.py:73
  207.0 13.2 %fusion.53 = (f32[1,20,128,256]{3,2,0,1:T(8,128)S(1)}, f32[1,20,128,256]{3,2,0,1:T(8,128)S(1)}) fusion(f32[4,20,128,256]{3,2,1,0:T(8,128)} %get-tuple-element.73, f32[4,20,128,256]{3,2,1,0:T(8,128)} %get-tuple-element.72, f32[20,130,258]{2,1,0:T(8,128)} %add_multiply_fusion, f32[4,20,130,258]{3,2,1,0:T(8,128)} %scatter.4, f32[128]{0:T(128)S(1)} %get-tuple-element.100, ...), kind=kLoop, calls=%fused_computation.109 | loop fusion | flops 11796480 | bytes 31458304 | tf_op jit(solution)/shard_map/broadcast_in_dim | solution.py:87
  220.7 10.6 %pad_maximum_fusion.2 = f32[4,20,128,256]{3,2,0,1:T(8,128)} fusion(f32[1,20,128,256]{3,2,0,1:T(8,128)S(1)} %get-tuple-element.71, f32[1,20,128,256]{3,2,0,1:T(8,128)S(1)} %get-tuple-element.70, f32[4,20,128,256]{3,2,1,0:T(8,128)} %get-tuple-element.73, f32[4,20,128,256]{3,2,1,0:T(8,128)S(1)} %copy-done.2, f32[4,20,130,258]{3,2,1,0:T(8,128)} %scatter.4), kind=kLoop, calls=%fused_computation.50 | loop fusion | flops 10485760 | bytes 31457280 | tf_op jit(solution)/shard_map/concatenate | solution.py:87
  231.3 26.1 %fusion.126 = f32[4,20,128,256]{3,2,0,1:T(8,128)} fusion(f32[4,20,128,256]{3,2,0,1:T(8,128)} %pad_maximum_fusion.2, s32[16384]{0:T(1024)S(1)} %bitcast.180, pred[16384]{0:T(1024)(128)(4,1)S(1)} %copy-done.20, f32[4,16384]{1,0:T(4,128)S(1)} %bitcast.169, f32[128,16384]{1,0:T(8,128)} %copy-done.4), kind=kOutput, calls=%fused_computation.181 | convolution fusion | flops 25786843136 | bytes 9781248 | tf_op jit(solution)/shard_map/dot_general | solution.py:153
  257.4 5.6 %fusion.41 = f32[20,128,256]{2,1,0:T(8,128)} fusion(f32[4,20,128,256]{3,2,0,1:T(8,128)} %fusion.126, f32[128,256,20]{1,2,0:T(8,128)S(1)} %copy-done.3), kind=kLoop, calls=%fused_computation.92 | loop fusion | flops 5242880 | bytes 10485760 | tf_op jit(solution)/shard_map/div | solution.py:115
  263.0 8.7 %fusion.181 = (f32[2,20,128,256]{3,2,0,1:T(8,128)S(1)}, f32[2,20,128,256]{3,2,0,1:T(8,128)}) fusion(f32[4,20,128,256]{3,2,0,1:T(8,128)} %fusion.126, f32[20,128,256]{2,1,0:T(8,128)} %fusion.41), kind=kLoop, calls=%fused_computation.265 | loop fusion | flops 1310720 | bytes 23592960 | tf_op jit(solution)/shard_map/slice | solution.py:116
  271.7 4.2 %fusion.107 = (f32[4,1,128,256]{3,2,0,1:T(8,128)S(1)}, f32[4,1,128,256]{3,2,0,1:T(8,128)S(1)}, f32[4,1,128,256]{3,2,0,1:T(8,128)S(1)}, f32[4,1,128,256]{3,2,0,1:...) fusion(f32[2,20,128,256]{3,2,0,1:T(8,128)} %get-tuple-element.8, ...), kind=kLoop, calls=%fused_computation.160 | loop fusion | flops 6815744 | bytes 19398656 | tf_op jit(solution)/shard_map/add | solution.py:103
  276.6 3.8 %subtract_dynamic-update-slice_fusion = (f32[4,20,128,256]{3,2,0,1:T(8,128)}, f32[4,1,128,256]{3,2,0,1:T(8,128)S(1)}, f32[4,1,128,256]{3,2,0,1:T(8,128)S(1)}, f3...) fusion(f32[4,1,128,256]{3,2,0,1:T(8,128)S(1)} %get-tuple-elemen, ...), kind=kLoop, calls=%fused_computation.183 | loop fusion | flops 8388607 | bytes 25165824
  280.4 1.0 constant_dynamic-update-slice_fusion.8
  281.3 0.9 fusion.140
  283.0 0.9 fusion.139
  284.8 0.9 fusion.138
  286.5 0.9 fusion.137
  290.0 0.9 fusion.135
  291.7 0.9 fusion.134
  293.5 0.9 fusion.133
  295.3 0.9 fusion.132
  297.0 9.4 %copy.70 = f32[4,20,128,256]{3,2,1,0:T(8,128)} copy(f32[4,20,128,256]{3,2,0,1:T(8,128)} %multiply_dynamic-update-slice_fusion) | data formatting | bytes 20971520
  (101 shorter events, 13.2 us)
Async XLA Ops:
  0.6 55.5 %copy-start = (f32[8,20]{1,0:T(8,128)S(1)}, f32[8,20]{1,0:T(8,128)}, u32[]{:S(2)}) copy-start(f32[8,20]{1,0:T(8,128)} %param.17) | copy-start | bytes 1924
  0.6 14.2 %slice-start.2 = ((f32[4,20,128,256]{3,2,1,0:T(8,128)}), f32[4,1,128,256]{3,2,1,0:T(8,128)S(1)}, s32[]{:S(2)}) async-start(f32[4,20,128,256]{3,2,1,0:T(8,128)} %param.15), calls=%async_computation.4 | async-start | bytes 1048576 | tf_op jit(solution)/shard_map/slice | solution.py:186
  2.1 58.2 %collective-permute-start.1 = (f32[4,20,1,256]{3,2,1,0:T(1,128)S(1)}, f32[4,20,1,256]{3,2,1,0:T(1,128)S(1)}, u32[]{:S(2)}, u32[]{:S(2)}) collective-permute-start(f32[4,20,1,256]{3,2,1,0:T(1,128)S(1)} %get-tuple-element.83), channel_id=1, source_target_pairs={{1,0},{2,1},{3,2},{4,3},{5,4},{6,5},{7,6},{9,8},{10,9},{11,10},{12... | collective-permute-start | bytes 245768 | tf_op jit(solution)/shard_map/ppermute | solution.py:32
  5.5 54.8 %collective-permute-start = (f32[4,20,1,256]{3,2,1,0:T(1,128)S(1)}, f32[4,20,1,256]{3,2,1,0:T(1,128)}, u32[]{:S(2)}, u32[]{:S(2)}) collective-permute-start(f32[4,20,1,256]{3,2,1,0:T(1,128)S(1)} %get-tuple-element.82), channel_id=1, source_target_pairs={{0,1},{1,2},{2,3},{3,4},{4,5},{5,6},{6,7},{8,9},{9,10},{10,11},{11... | collective-permute-start | bytes 245768 | tf_op jit(solution)/shard_map/ppermute | solution.py:31
  9.6 77.5 %collective-permute-start.4 = (f32[4,20,256]{2,0,1:T(4,128)}, f32[4,20,256]{2,0,1:T(4,128)}, u32[]{:S(2)}, u32[]{:S(2)}) collective-permute-start(f32[4,20,256]{2,0,1:T(4,128)} %rev.3), channel_id=1, source_target_pairs={{0,8},{8,0},{16,24},{24,16},{32,40},{40,32},{48,56},{56,48},{64,72... | collective-permute-start | bytes 245768 | tf_op jit(solution)/shard_map/ppermute | solution.py:44
  13.4 18.0 %copy-start.19 = (pred[16384]{0:T(1024)(128)(4,1)}, pred[16384]{0:T(1024)(128)(4,1)S(1)}, u32[]{:S(2)}) copy-start(pred[16384]{0:T(1024)(128)(4,1)S(1)} %compare_reduce_fusion) | copy-start | bytes 49156
  13.5 17.9 %copy-start.23 = (s32[1,16384]{1,0:T(1,128)}, s32[1,16384]{1,0:T(1,128)S(1)}, u32[]{:S(2)}) copy-start(s32[1,16384]{1,0:T(1,128)S(1)} %and_select_fusion.1) | copy-start | bytes 196612
  13.5 27.7 %copy-start.6 = (s32[1,16384]{1,0:T(1,128)S(1)}, s32[1,16384]{1,0:T(1,128)}, u32[]{:S(2)}) copy-start(s32[1,16384]{1,0:T(1,128)} %param.19) | copy-start | bytes 196612
  14.8 16.7 %copy-start.4 = (f32[128,16384]{1,0:T(8,128)}, f32[128,16384]{1,0:T(8,128)S(1)}, u32[]{:S(2)}) copy-start(f32[128,16384]{1,0:T(8,128)S(1)} %fusion.17) | copy-start | bytes 25165828
  14.8 27.2 %copy-start.21 = (f32[1,2,8192]{2,1,0:T(2,128)S(1)}, f32[1,2,8192]{2,1,0:T(2,128)}, u32[]{:S(2)}) copy-start(f32[1,2,8192]{2,1,0:T(2,128)} %param.24) | copy-start | bytes 196612
  14.8 30.6 %copy-start.16 = (f32[1,8192]{1,0:T(1,128)S(1)}, f32[1,8192]{1,0:T(1,128)}, u32[]{:S(2)}) copy-start(f32[1,8192]{1,0:T(1,128)} %param.22) | copy-start | bytes 98308
  14.8 30.6 %copy-start.25 = (f32[1,8192]{1,0:T(1,128)S(1)}, f32[1,8192]{1,0:T(1,128)}, u32[]{:S(2)}) copy-start(f32[1,8192]{1,0:T(1,128)} %param.23) | copy-start | bytes 98308
  31.4 84.6 %all-to-all-start = ((f32[4,128,128]{2,0,1:T(4,128)}), f32[4,128,128]{2,0,1:T(4,128)S(1)}, u32[]{:S(2)}, u32[]{:S(2)}) async-start(f32[4,128,128]{2,0,1:T(4,128)} %bitcast.33), calls=%async_computation | async-start | bytes 524288 | tf_op jit(solution)/shard_map/all_to_all | solution.py:190
  41.7 13.5 %copy-start.10 = (pred[16384]{0:T(1024)(128)(4,1)}, pred[16384]{0:T(1024)(128)(4,1)S(1)}, u32[]{:S(2)}) copy-start(pred[16384]{0:T(1024)(128)(4,1)S(1)} %compare_reduce_fusion.1) | copy-start | bytes 49156
  42.0 3.4 %copy-start.12 = (s32[1,16384]{1,0:T(1,128)}, s32[1,16384]{1,0:T(1,128)S(1)}, u32[]{:S(2)}) copy-start(s32[1,16384]{1,0:T(1,128)S(1)} %and_select_fusion.2) | copy-start | bytes 196612
  42.6 13.4 %copy-start.18 = (s32[128,256]{1,0:T(8,128)S(1)}, s32[128,256]{1,0:T(8,128)}, u32[]{:S(2)}) copy-start(s32[128,256]{1,0:T(8,128)} %param.16) | copy-start | bytes 393220
  45.4 13.8 %copy-start.22 = (s32[1,16384]{1,0:T(1,128)S(1)}, s32[1,16384]{1,0:T(1,128)}, u32[]{:S(2)}) copy-start(s32[1,16384]{1,0:T(1,128)} %param.20) | copy-start | bytes 196612
  45.4 13.8 %copy-start.26 = (f32[64]{0:T(128)S(1)}, f32[64]{0:T(128)}, u32[]{:S(2)}) copy-start(f32[64]{0:T(128)} %param.21) | copy-start | bytes 772
  76.5 10.7 %collective-permute-start.3 = (f32[4,20,130,1]{2,0,3,1:T(4,128)S(1)}, f32[4,20,130,1]{2,0,3,1:T(4,128)S(1)}, u32[]{:S(2)}, u32[]{:S(2)}) collective-permute-start(f32[4,20,130,1]{2,0,3,1:T(4,128)S(1)} %copy.56), channel_id=1, source_target_pairs={{8,0},{16,8},{24,16},{32,24},{40,32},{48,40},{56,48},{64,56},{72,6... | collective-permute-start | bytes 124808 | tf_op jit(solution)/shard_map/ppermute | solution.py:32
  86.9 7.2 %collective-permute-start.2 = (f32[4,20,130,1]{2,0,3,1:T(4,128)S(1)}, f32[4,20,130,1]{2,0,3,1:T(4,128)S(1)}, u32[]{:S(2)}, u32[]{:S(2)}) collective-permute-start(f32[4,20,130,1]{2,0,3,1:T(4,128)S(1)} %copy.55), channel_id=1, source_target_pairs={{0,8},{8,16},{16,24},{24,32},{32,40},{40,48},{48,56},{56,64},{64,7... | collective-permute-start | bytes 124808 | tf_op jit(solution)/shard_map/ppermute | solution.py:31
  87.0 10.5 %collective-permute-start.5 = (f32[4,20,256]{2,0,1:T(4,128)}, f32[4,20,256]{2,0,1:T(4,128)S(1)}, u32[]{:S(2)}, u32[]{:S(2)}) collective-permute-start(f32[4,20,256]{2,0,1:T(4,128)} %collective-permute-done.4), channel_id=1, source_target_pairs={{0,16},{16,0},{8,24},{24,8},{32,48},{48,32},{40,56},{56,40},{64,80... | collective-permute-start | bytes 245768 | tf_op jit(solution)/shard_map/ppermute | solution.py:44
  97.5 18.7 %copy-start.7 = (f32[128,128]{1,0:T(8,128)S(1)}, f32[128,128]{1,0:T(8,128)}, u32[]{:S(2)}) copy-start(f32[128,128]{1,0:T(8,128)} %select_reduce_fusion) | copy-start | bytes 196612
  97.5 18.7 %copy-start.8 = (f32[1,16384]{1,0:T(1,128)S(1)}, f32[1,16384]{1,0:T(1,128)}, u32[]{:S(2)}) copy-start(f32[1,16384]{1,0:T(1,128)} %get-tuple-element.90) | copy-start | bytes 196612
  97.5 18.7 %copy-start.9 = (f32[1,16384]{1,0:T(1,128)S(1)}, f32[1,16384]{1,0:T(1,128)}, u32[]{:S(2)}) copy-start(f32[1,16384]{1,0:T(1,128)} %get-tuple-element.93) | copy-start | bytes 196612
  97.5 18.7 %copy-start.14 = (f32[1,16384]{1,0:T(1,128)S(1)}, f32[1,16384]{1,0:T(1,128)}, u32[]{:S(2)}) copy-start(f32[1,16384]{1,0:T(1,128)} %get-tuple-element.91) | copy-start | bytes 196612
  97.5 18.7 %copy-start.15 = (f32[1,16384]{1,0:T(1,128)S(1)}, f32[1,16384]{1,0:T(1,128)}, u32[]{:S(2)}) copy-start(f32[1,16384]{1,0:T(1,128)} %get-tuple-element.92) | copy-start | bytes 196612
  97.5 29.1 %copy-start.5 = (pred[128,16384]{1,0:T(32,128)(4,1)S(1)}, pred[128,16384]{1,0:T(32,128)(4,1)}, u32[]{:S(2)}) copy-start(pred[128,16384]{1,0:T(32,128)(4,1)} %fusion.196) | copy-start | bytes 6291460
  97.5 29.1 %copy-start.11 = (pred[16384]{0:T(1024)(128)(4,1)S(1)}, pred[16384]{0:T(1024)(128)(4,1)}, u32[]{:S(2)}) copy-start(pred[16384]{0:T(1024)(128)(4,1)} %copy-done.10) | copy-start | bytes 49156
  97.5 29.0 %copy-start.13 = (s32[1,16384]{1,0:T(1,128)S(1)}, s32[1,16384]{1,0:T(1,128)}, u32[]{:S(2)}) copy-start(s32[1,16384]{1,0:T(1,128)} %copy-done.12) | copy-start | bytes 196612
  97.5 34.3 %copy-start.17 = (f32[1,8192]{1,0:T(1,128)S(1)}, f32[1,8192]{1,0:T(1,128)}, u32[]{:S(2)}) copy-start(f32[1,8192]{1,0:T(1,128)} %param.22) | copy-start | bytes 98308
  97.6 35.0 %copy-start.27 = (f32[4]{0:T(128)S(1)}, f32[4]{0:T(128)}, u32[]{:S(2)}) copy-start(f32[4]{0:T(128)} %constant.237.clone) | copy-start | bytes 52
  97.6 17.9 %collective-permute-start.6 = (f32[4,20,256]{2,0,1:T(4,128)S(1)}, f32[4,20,256]{2,0,1:T(4,128)}, u32[]{:S(2)}, u32[]{:S(2)}) collective-permute-start(f32[4,20,256]{2,0,1:T(4,128)S(1)} %collective-permute-done.5), channel_id=1, source_target_pairs={{0,32},{32,0},{8,40},{40,8},{16,48},{48,16},{24,56},{56,24},{64,96... | collective-permute-start | bytes 245768 | tf_op jit(solution)/shard_map/ppermute | solution.py:44
  115.4 17.1 %collective-permute-start.7 = (f32[4,20,256]{2,0,1:T(4,128)}, f32[4,20,256]{2,0,1:T(4,128)S(1)}, u32[]{:S(2)}, u32[]{:S(2)}) collective-permute-start(f32[4,20,256]{2,0,1:T(4,128)} %collective-permute-done.6), channel_id=1, source_target_pairs={{0,64},{64,0},{8,72},{72,8},{16,80},{80,16},{24,88},{88,24},{32,96... | collective-permute-start | bytes 245768 | tf_op jit(solution)/shard_map/ppermute | solution.py:44
  117.2 114.1 %all-to-all-start.1 = ((f32[4,128,128]{2,0,1:T(4,128)}), f32[4,128,128]{2,0,1:T(4,128)S(1)}, u32[]{:S(2)}, u32[]{:S(2)}) async-start(f32[4,128,128]{2,0,1:T(4,128)} %copy.68), calls=%async_computation.1 | async-start | bytes 524288 | tf_op jit(solution)/shard_map/all_to_all | solution.py:211
  207.0 13.7 %copy-start.2 = (f32[4,20,128,256]{3,2,1,0:T(8,128)S(1)}, f32[4,20,128,256]{3,2,1,0:T(8,128)}, u32[]{:S(2)}) copy-start(f32[4,20,128,256]{3,2,1,0:T(8,128)} %get-tuple-element.72) | copy-start | bytes 31457284
  220.7 10.6 %copy-start.20 = (pred[16384]{0:T(1024)(128)(4,1)S(1)}, pred[16384]{0:T(1024)(128)(4,1)}, u32[]{:S(2)}) copy-start(pred[16384]{0:T(1024)(128)(4,1)} %copy-done.19) | copy-start | bytes 49156
  220.7 10.6 %copy-start.24 = (s32[1,16384]{1,0:T(1,128)S(1)}, s32[1,16384]{1,0:T(1,128)}, u32[]{:S(2)}) copy-start(s32[1,16384]{1,0:T(1,128)} %copy-done.23) | copy-start | bytes 196612
  231.3 26.1 %copy-start.3 = (f32[128,256,20]{1,2,0:T(8,128)S(1)}, f32[128,256,20]{1,2,0:T(8,128)}, u32[]{:S(2)}) copy-start(f32[128,256,20]{1,2,0:T(8,128)} %fusion.85) | copy-start | bytes 7864324
  271.7 4.4 %slice-start = ((s8[5242880]{0:T(1024)(128)(4,1)}), s8[4194304]{0:T(1024)(128)(4,1)S(1)}, s32[]{:S(2)}) async-start(s8[5242880]{0:T(1024)(128)(4,1)} %bitcast.154), calls=%async_computation.2 | async-start | bytes 8388608
  271.7 4.9 %slice-start.1 = ((s8[5242880]{0:T(1024)(128)(4,1)}), s8[1048576]{0:T(1024)(128)(4,1)S(1)}, s32[]{:S(2)}) async-start(s8[5242880]{0:T(1024)(128)(4,1)} %bitcast.154), calls=%async_computation.3 | async-start | bytes 2097152
  296.1 10.2 %copy-start.1 = (f32[8,20]{1,0:T(8,128)S(1)}, f32[8,20]{1,0:T(8,128)}, u32[]{:S(2)}) copy-start(f32[8,20]{1,0:T(8,128)} %param.17) | copy-start | bytes 1924
where the time goes:
time: 313 us; the launch traced here: 307 us
  other arithmetic  147 us (47%)
  matrix products  60.8 us (19%)
  local copies, waits for them, and re-layouts  60.1 us (19%)
  starting transfers between devices  33.8 us (11%)
  waiting for transfers between devices  3.56 us (1%)
    sub x1, other arithmetic, provisional(): laplace = east_side + west_side + north_side + south_side - 4.0 * centre  37.1 us
    dot_general x2, matrix products, spread_slots(): lax.dot_general(weighted, low_hot, (((1,), (1,)), ((), ())), precision=la...  31.4 us
    dot_general x2, matrix products, pick_slots(): jnp.dot(table.reshape(fields * high_count, low_count), low_hot, precision...  26.4 us
    concatenate x2, other arithmetic, extended_2(): array = jnp.concatenate([before, array, after], axis=dim)  23.1 us
    unnamed x69, local copies, waits for them, and re-layouts  17.5 us
    scatter x1, local copies, waits for them, and re-layouts, shards(): extended = extended.at[:, :, block_rows + 1, 1:-1].set(folded)  15.6 us
    broadcast_in_dim x1, other arithmetic, provisional(): return jnp.concatenate([tracers, u_next[None], v_next[None]], axis=0)  13.2 us
    unnamed x12, other arithmetic  12.7 us
  transfers between devices with their start and end apart: 10, of which 1 were waited for; matrix products, arithmetic and copies ran while one was open for 62% of the time, Pallas kernels for 0%

commit v1 on v0

v1 whole, which is shorter than its diff:
```python
import functools

import jax
import jax.numpy as jnp
from jax import lax
from jax.experimental import pallas as pl
from jax.experimental.pallas import tpu as pltpu
from jax.sharding import PartitionSpec as P

f32 = jnp.float32
bf16 = jnp.bfloat16
i32 = jnp.int32
MESH = pl.DeviceIdType.MESH
K = 20
NF = 4
FK = NF * K
CJ = 128
CI = 256
NLON = 16
NLAT = 8
DEV = NLON * NLAT
SLOTS = 128
ROWS = 8
SENT = 6
SCALE = 40.0

DIAG = [1.5]
for _k in range(1, K):
    DIAG.append((1.5 if _k == K - 1 else 2.0) - 0.25 / DIAG[-1])
FWD = [0.0] + [0.5 / DIAG[_k - 1] for _k in range(1, K)]
TOP = [1.0]
for _k in range(1, K):
    TOP.append(FWD[_k] * TOP[-1])

VM = pl.BlockSpec(memory_space=pltpu.VMEM)
ANY = pl.BlockSpec(memory_space=pl.ANY)
LIMIT = 60 << 20


def lanes():
    return lax.broadcasted_iota(i32, (8, 128), 1)


def take(table, index, axis):
    return jnp.take_along_axis(table, index, axis=axis, mode="promise_in_bounds")


def split(x):
    high = x.astype(bf16)
    return high, (x - high.astype(f32)).astype(bf16)


def one_hot(index, count):
    rows = lax.broadcasted_iota(i32, (count, index.shape[1]), 0)
    return rows == jnp.broadcast_to(index, (count, index.shape[1]))


def pack(even, odd):
    left = lanes() < 64
    return (
        jnp.where(left, even, pltpu.roll(odd, 64, 1)),
        jnp.where(left, pltpu.roll(even, 64, 1), odd),
    )


def pack_list(source, packed):
    for g in range(8):
        first, second = pack(
            source[pl.ds(16 * g, 8, stride=2), :], source[pl.ds(16 * g + 1, 8, stride=2), :]
        )
        packed[8 * g : 8 * g + 8, :] = first
        packed[64 + 8 * g : 72 + 8 * g, :] = second


def long_pairs(flags, first, count):
    most = flags[first, 64]
    for i in range(1, count):
        most = jnp.maximum(most, flags[first + i, 64])
    return most >= 0


def gather_kernel(
    st, olist_any, ilist_any, olist, ilist, wlist, area, itemp, icond, ivel,
    out, tuv, rowlo, rowhi, colw, cole,
    full, otab, itab, opack, ipack, ogot, igot, oflag, iflag, sems,
):
    flags = [
        pltpu.make_async_copy(olist_any, oflag, sems.at[0]),
        pltpu.make_async_copy(ilist_any, iflag, sems.at[1]),
    ]
    loads = []
    for n, f in enumerate((0, 2, 3, 1)):
        loads.append([
            pltpu.make_async_copy(
                st.at[f * K : (f + 1) * K, :, c * 128 : (c + 1) * 128],
                full.at[c, f * K : (f + 1) * K],
                sems.at[2 + 2 * n + c],
            )
            for c in range(2)
        ])
    for copy in flags:
        copy.start()
    for pair in loads:
        for copy in pair:
            copy.start()
    pack_list(olist, opack)
    pack_list(ilist, ipack)
    ogot[...] = jnp.zeros_like(ogot)
    igot[...] = jnp.zeros_like(igot)
    for f in range(4):
        for c in range(2):
            if f < 2:
                x = (icond, itemp)[f][pl.ds(c, 32, stride=2), :]
            else:
                x = ivel[pl.ds(2 * c + f - 2, 32, stride=4), :]
            high, low = split(x)
            itab[32 * f : 32 * f + 32, c * 128 : (c + 1) * 128] = high
            itab[128 + 32 * f : 160 + 32 * f, c * 128 : (c + 1) * 128] = low

    def gather(tile, packed, table, fields, rows, got):
        hots, his = [], []
        for h in range(2):
            row = packed[pl.ds(2 * tile + h, 1), :]
            his.append(row >> 8)
            hots.append(jnp.where(one_hot(row & 255, 256), 1.0, 0.0).astype(bf16))
        res = jnp.dot(table[...], jnp.concatenate(hots, axis=1), preferred_element_type=f32)
        half = fields * rows
        res = res[:half] + res[half:]
        for h in range(2):
            mask = one_hot(his[h], rows)
            for f in range(fields):
                value = jnp.where(mask, res[f * rows : (f + 1) * rows, h * 128 : (h + 1) * 128], 0.0)
                got[pl.ds(f * 128 + 2 * tile + h, 1), :] = jnp.sum(value, axis=0, keepdims=True)

    @pl.loop(0, 32, step=4)
    def _(t):
        for j in range(4):
            gather(t + j, ipack, itab, 4, 32, igot)

    for copy in flags:
        copy.wait()

    @pl.loop(0, 32)
    def _(t):
        @pl.when(long_pairs(iflag, 4 * t, 4))
        def _():
            gather(32 + t, ipack, itab, 4, 32, igot)

    for n in range(3):
        for copy in loads[n]:
            copy.wait()
    for n, f in enumerate((0, 2, 3)):
        for c in range(2):
            high, low = split(full[c, f * K])
            otab[128 * n : 128 * n + 128, c * 128 : (c + 1) * 128] = high
            otab[384 + 128 * n : 512 + 128 * n, c * 128 : (c + 1) * 128] = low

    @pl.loop(0, 32, step=2)
    def _(t):
        for j in range(2):
            gather(t + j, opack, otab, 3, 128, ogot)

    @pl.loop(0, 32)
    def _(t):
        @pl.when(long_pairs(oflag, 4 * t, 4))
        def _():
            gather(32 + t, opack, otab, 3, 128, ogot)

    left = lanes() < 64

    def unpack(got, f, g):
        first = got[f * 128 + 8 * g : f * 128 + 8 * g + 8, :]
        second = got[f * 128 + 64 + 8 * g : f * 128 + 72 + 8 * g, :]
        return (
            jnp.where(left, first, pltpu.roll(second, 64, 1)),
            jnp.where(left, pltpu.roll(first, 64, 1), second),
        )

    areas = jnp.broadcast_to(jnp.concatenate([area[...], area[...]], axis=1), (8, 128))
    for g in range(8):
        for n in range(3):
            even, odd = unpack(ogot, n, g)
            tuv[pl.ds(128 * n + 16 * g, 8, stride=2), :] = even
            tuv[pl.ds(128 * n + 16 * g + 1, 8, stride=2), :] = odd
            if n == 0:
                out[pl.ds(128 * g, 8, stride=16), :] = even
                out[pl.ds(128 * g + 8, 8, stride=16), :] = odd
        for f in range(4):
            even, odd = unpack(igot, f, g)
            out[pl.ds(128 * g + 2 + f, 8, stride=16), :] = even
            out[pl.ds(128 * g + 10 + f, 8, stride=16), :] = odd
    for g in range(16):
        index = wlist[8 * g : 8 * g + 8, :]
        value = jnp.where(index >= 0, take(areas, index & 63, 1), 0.0)
        out[pl.ds(64 * g + 1, 8, stride=8), :] = value
        for f in range(SENT, ROWS):
            out[pl.ds(64 * g + f, 8, stride=8), :] = jnp.zeros((8, 128), f32)

    for copy in loads[3]:
        copy.wait()
    for fk in range(FK):
        for c in range(2):
            rowlo[fk : fk + 1, c * 128 : (c + 1) * 128] = full[c, fk, 0:1, :]
            rowhi[fk : fk + 1, c * 128 : (c + 1) * 128] = full[c, fk, 127:128, :]

    @pl.loop(0, 16)
    def _(m):
        lane = lanes()
        rows = pl.ds(pl.multiple_of(8 * m, 8), 8)
        west = jnp.zeros((8, 128), f32)
        east = jnp.zeros((8, 128), f32)
        for fk in range(FK):
            both = jnp.where(lane == 127, full[1, fk, rows, :], full[0, fk, rows, :])
            both = pltpu.roll(both, fk, 1) if fk else both
            west = jnp.where(lane == fk, both, west)
            east = jnp.where(lane == (fk - 1) % 128, both, east)
        colw[rows, :] = west
        cole[rows, :] = east


def stencil_row(m, buf, q, canopy, east_col, west_col, drag, lat):
    lane = lanes()
    sub = lax.broadcasted_iota(i32, (8, 128), 0)
    first, last = lane == 0, lane == 127
    rows = pl.ds(pl.multiple_of(8 * m, 8), 8)
    east_halo, west_halo = east_col[rows, :], west_col[rows, :]
    kind = [canopy[rows, c * 128 : (c + 1) * 128] for c in range(2)]
    row = (lat * CJ + 8 * m + sub).astype(f32)
    cor = 4.0 * (2.0 * (row + 0.5) / (CJ * NLAT) - 1.0)
    elim = [[None] * 2 for _ in range(NF)]
    gx, gy = [None] * 2, [None] * 2
    for k in range(K):
        C, E, W, N, S = ([[None] * 2 for _ in range(NF)] for _ in range(5))
        for f in range(NF):
            fk = f * K + k
            for c in range(2):
                C[f][c] = buf[c, fk, pl.ds(pl.multiple_of(8 + 8 * m, 8), 8), :]
                N[f][c] = buf[c, fk, pl.ds(9 + 8 * m, 8), :]
                S[f][c] = buf[c, fk, pl.ds(7 + 8 * m, 8), :]
            e0, e1 = (pltpu.roll(C[f][c], 127, 1) for c in range(2))
            w0, w1 = (pltpu.roll(C[f][c], 1, 1) for c in range(2))
            E[f][0] = jnp.where(last, e1, e0)
            E[f][1] = jnp.where(last, pltpu.roll(east_halo, (127 - fk) % 128, 1), e1)
            W[f][0] = jnp.where(first, pltpu.roll(west_halo, (1 - fk) % 128, 1), w0)
            W[f][1] = jnp.where(first, w0, w1)
        for c in range(2):
            u, v = C[2][c], C[3][c]
            eE = (0.4 - u) - E[2][c]
            eW = (0.4 + u) + W[2][c]
            eN = (0.4 - v) - N[3][c]
            eS = (0.4 + v) + S[3][c]
            mid = 36.8 + ((eE + eW) + (eN + eS))
            new = [
                (C[f][c] * mid + E[f][c] * eE) + (W[f][c] * eW + N[f][c] * eN) + S[f][c] * eS
                for f in range(NF)
            ]
            hx = 0.4 * (E[1][c] - W[1][c]) - 0.1 * (E[0][c] - W[0][c])
            hy = 0.4 * (N[1][c] - S[1][c]) - 0.1 * (N[0][c] - S[0][c])
            px = hx if k == 0 else gx[c] + hx
            py = hy if k == 0 else gy[c] + hy
            gx[c], gy[c] = px + hx, py + hy
            new[2] = new[2] + (cor * v - px)
            new[3] = new[3] - (cor * u + py)
            if k > 0:
                x = new[2] * new[2] + (new[3] * new[3] + 0.01 * SCALE * SCALE)
                damp = 1.0 / (1.0 + take(drag[k], kind[c], 0) * (x * lax.rsqrt(x)))
                new[2], new[3] = new[2] * damp, new[3] * damp
            for f in range(NF):
                if k > 1:
                    new[f] = new[f] + FWD[k] * elim[f][c]
                elim[f][c] = new[f]
                q[m, f * K + k, c * 8 : (c + 1) * 8, :] = new[f]


def drag_levels(table, drag):
    for k in range(K):
        drag[k] = jnp.broadcast_to(table[:, k : k + 1] * (0.1 / SCALE), (8, 128))


def stencil_kernel(
    st, out, canopy, table, rowlo, rowhi, colw, cole,
    q, inb,
    buf, drag, mid, north, south, east_col, west_col, sems, hops, halo_send, halo_recv,
):
    lon, lat = lax.axis_index("lon"), lax.axis_index("lat")
    loads = [
        [
            pltpu.make_async_copy(
                st.at[:, 32 * g : 32 * g + 32, c * 128 : (c + 1) * 128],
                buf.at[c, :, 8 + 32 * g : 40 + 32 * g, :],
                sems.at[g, c],
            )
            for c in range(2)
        ]
        for g in range(4)
    ]
    for pair in loads:
        for copy in pair:
            copy.start()

    barrier = pltpu.get_barrier_semaphore()
    for i in range(1, NLON):
        pl.semaphore_signal(barrier, inc=1, device_id=(lax.rem(lon + i, NLON), lat), device_id_type=MESH)
    for i in range(1, NLAT):
        pl.semaphore_signal(barrier, inc=1, device_id=(lon, lax.rem(lat + i, NLAT)), device_id_type=MESH)
    pl.semaphore_wait(barrier, NLON + NLAT - 2)

    def halo(src, dst, n, target):
        return pltpu.make_async_remote_copy(
            src_ref=src, dst_ref=dst, send_sem=halo_send.at[n], recv_sem=halo_recv.at[n],
            device_id=target, device_id_type=MESH,
        )

    to_west = halo(colw, east_col, 0, (lax.rem(lon + NLON - 1, NLON), lat))
    to_east = halo(cole, west_col, 1, (lax.rem(lon + 1, NLON), lat))
    to_north = halo(rowhi, south, 2, (lon, lax.rem(lat + 1, NLAT)))
    to_south = halo(rowlo, north, 3, (lon, lax.rem(lat + NLAT - 1, NLAT)))
    to_fold = halo(rowhi, north, 3, (NLON - 1 - lon, lat))
    to_west.start()
    to_east.start()
    to_north.start()

    @pl.when(lat > 0)
    def _():
        to_south.start()

    @pl.when(lat == NLAT - 1)
    def _():
        pltpu.make_async_remote_copy(
            src_ref=rowhi, dst_ref=north, send_sem=halo_send.at[4], recv_sem=halo_recv.at[3],
            device_id=(NLON - 1 - lon, lat), device_id_type=MESH,
        ).start()

    for i in range(1, NLON):
        peer = lax.rem(lon + i, NLON)
        pltpu.make_async_remote_copy(
            src_ref=out.at[pl.ds(peer * NLAT, NLAT)], dst_ref=mid.at[pl.ds(lon * NLAT, NLAT)],
            send_sem=hops.at[0], recv_sem=hops.at[1], device_id=(peer, lat), device_id_type=MESH,
        ).start()
    own = pltpu.make_async_copy(out.at[pl.ds(lon * NLAT, NLAT)], mid.at[pl.ds(lon * NLAT, NLAT)], hops.at[2])
    own.start()

    drag_levels(table, drag)
    to_west.wait_recv()
    to_east.wait_recv()
    to_north.wait_recv()
    to_fold.wait_recv()
    top = lat == NLAT - 1
    inside = jnp.where(lat > 0, 1.0, 0.0)
    back = 127 - lanes()
    for g in range(10):
        part = slice(8 * g, 8 * g + 8)
        sign = 1.0 if g < 5 else -1.0
        halves = [north[part, c * 128 : (c + 1) * 128] for c in range(2)]
        for c in range(2):
            turned = sign * take(halves[1 - c], back, 1)
            value = jnp.where(top, turned, halves[c])
            below = south[part, c * 128 : (c + 1) * 128] * inside
            for r in range(8):
                buf[c, 8 * g + r, 136:137, :] = value[r : r + 1]
                buf[c, 8 * g + r, 7:8, :] = below[r : r + 1]
    for copy in loads[0]:
        copy.wait()

    @pl.loop(0, 4)
    def _(g):
        @pl.when(g < 3)
        def _():
            for c in range(2):
                pltpu.make_async_copy(
                    st.at[:, 0:32, 0:128], buf.at[c, :, 8:40, :], sems.at[g + 1, c]
                ).wait()

        @pl.when(g == 2)
        def _():
            many = mid.at[0 : (NLON - 1) * NLAT]
            pltpu.make_async_copy(many, many, hops.at[1]).wait()
            own.wait()
            mid4 = mid.reshape(NLON, NLAT, ROWS, 128)
            in4 = inb.reshape(NLON, NLAT, ROWS, 128)
            for i in range(1, NLAT):
                peer = lax.rem(lat + i, NLAT)
                pltpu.make_async_remote_copy(
                    src_ref=mid4.at[:, peer], dst_ref=in4.at[:, lat],
                    send_sem=hops.at[3], recv_sem=hops.at[4], device_id=(lon, peer), device_id_type=MESH,
                ).start()
            pltpu.make_async_copy(mid4.at[:, lat], in4.at[:, lat], hops.at[2]).start()

        @pl.loop(0, 4)
        def _(j):
            stencil_row(4 * g + j, buf, q, canopy, east_col, west_col, drag, lat)

    some = inb.at[0 : (NLAT - 1) * NLON]
    pltpu.make_async_copy(some, some, hops.at[4]).wait()
    pltpu.make_async_copy(some, some, hops.at[3]).wait()
    one = inb.at[0:NLON]
    pltpu.make_async_copy(one, one, hops.at[2]).wait()
    many = mid.at[0 : (NLON - 1) * NLAT]
    pltpu.make_async_copy(many, many, hops.at[0]).wait()
    to_west.wait_send()
    to_east.wait_send()
    to_north.wait_send()

    @pl.when(lat > 0)
    def _():
        to_south.wait_send()

    @pl.when(lat == NLAT - 1)
    def _():
        pltpu.make_async_copy(rowhi, rowhi, halo_send.at[4]).wait()


def finish_kernel(
    st, olist_any, ilist_any, q, inb, out, tuv, olist, ilist, canopy, table, itemp,
    y, itemp_next,
    ybuf, salt, drag, opack, ipack, oval, ival, oacc, iacc, wide, cols, oflag, iflag, sems,
):
    flags = [
        pltpu.make_async_copy(olist_any, oflag, sems.at[0]),
        pltpu.make_async_copy(ilist_any, iflag, sems.at[1]),
    ]
    salts = [
        pltpu.make_async_copy(st.at[K, :, c * 128 : (c + 1) * 128], salt.at[c], sems.at[2 + c])
        for c in range(2)
    ]
    for copy in flags + salts:
        copy.start()
    drag_levels(table, drag)
    pack_list(olist, opack)
    pack_list(ilist, ipack)
    for g in range(8):
        sides, ices = [], []
        for odd in range(2):
            block = lambda ref, f: ref[pl.ds(128 * g + 8 * odd + f, 8, stride=16), :]
            slot = [tuv[pl.ds(128 * n + 16 * g + odd, 8, stride=2), :] for n in range(3)]
            a, cond, temp, iu, iv = (block(inb, f) for f in range(1, 6))
            du, dv = iu - slot[1], iv - slot[2]
            x = du * du + dv * dv + 0.01
            drift = 0.5 * a * (x * lax.rsqrt(x))
            heat = a * cond
            sides.append([heat * (temp - slot[0]), heat, drift * du, drift * dv])
            ices.append(block(out, 1) * block(out, 2) * (block(out, 3) - block(inb, 0)))
        for f in range(4):
            first, second = pack(sides[0][f], sides[1][f])
            oval[128 * f + 8 * g : 128 * f + 8 * g + 8, :] = first
            oval[128 * f + 64 + 8 * g : 128 * f + 72 + 8 * g, :] = second
        first, second = pack(*ices)
        ival[8 * g : 8 * g + 8, :] = first
        ival[64 + 8 * g : 72 + 8 * g, :] = second
    oacc[...] = jnp.zeros_like(oacc)
    iacc[...] = jnp.zeros_like(iacc)

    def scatter(tile, packed, values, fields, rows, width, acc):
        for h in range(4):
            index = packed[pl.ds(4 * tile + h, 1), :]
            here = slice(128 * h, 128 * h + 128)
            cols[0:width, here] = jnp.where(one_hot(index & (width - 1), width), 1.0, 0.0).astype(bf16)
            mask = one_hot(index >> (width.bit_length() - 1), rows)
            for f in range(fields):
                value = values[pl.ds(128 * f + 4 * tile + h, 1), :]
                high = value.astype(bf16).astype(f32)
                for n, part in enumerate((high, value - high)):
                    part = jnp.where(mask, jnp.broadcast_to(part, (rows, 128)), 0.0).astype(bf16)
                    wide[rows * f : rows * (f + 1), 512 * n + 128 * h : 512 * n + 128 * h + 128] = part
        hot = cols[0:width, :]
        both = jnp.concatenate([hot, hot], axis=1)
        acc[...] += lax.dot_general(
            wide[0 : rows * fields, :], both, (((1,), (1,)), ((), ())), preferred_element_type=f32
        )

    def scatter_ocean(tile):
        scatter(tile, opack, oval, 4, CJ, CI, oacc)

    def scatter_ice(tile):
        scatter(tile, ipack, ival, 1, 64, 128, iacc)

    @pl.loop(0, 16)
    def _(t):
        scatter_ocean(t)

    @pl.loop(0, 16)
    def _(t):
        scatter_ice(t)

    for copy in flags:
        copy.wait()

    @pl.loop(0, 16)
    def _(t):
        @pl.when(long_pairs(oflag, 8 * t, 8))
        def _():
            scatter_ocean(16 + t)

        @pl.when(long_pairs(iflag, 8 * t, 8))
        def _():
            scatter_ice(16 + t)

    itemp_next[...] = itemp[...] - 0.25 * iacc[...]
    for copy in salts:
        copy.wait()

    @pl.loop(0, 16)
    def _(m):
        rows = pl.ds(pl.multiple_of(8 * m, 8), 8)
        sides = []
        for c in range(2):
            here = slice(8 * c, 8 * c + 8)
            flux = [
                oacc[pl.ds(pl.multiple_of(CJ * f + 8 * m, 8), 8), c * 128 : (c + 1) * 128] for f in range(4)
            ]
            top = [q[m, f * K, here, :] for f in range(4)]
            top[0] = top[0] + 20.0 * flux[0]
            top[1] = top[1] - 10.0 * (salt[c, rows, :] * flux[1])
            top[2] = top[2] + 20.0 * flux[2]
            top[3] = top[3] + 20.0 * flux[3]
            x = top[2] * top[2] + (top[3] * top[3] + 0.01 * SCALE * SCALE)
            damp = 1.0 / (1.0 + take(drag[0], canopy[rows, c * 128 : (c + 1) * 128], 0) * (x * lax.rsqrt(x)))
            top[2], top[3] = top[2] * damp, top[3] * damp
            sides.append(top)
        solved = [[None] * 4 for _ in range(2)]
        for k in range(K - 1, -1, -1):
            for c in range(2):
                for f in range(4):
                    here = slice(8 * c, 8 * c + 8)
                    value = sides[c][f] if k == 0 else q[m, f * K + k, here, :] + TOP[k] * sides[c][f]
                    value = value * (1.0 / (SCALE * DIAG[k]))
                    if k < K - 1:
                        value = value + (0.5 / DIAG[k]) * solved[c][f]
                    solved[c][f] = value
                    ybuf[m, f * K + k, here, :] = value
        for c in range(2):
            pltpu.make_async_copy(
                ybuf.at[m, :, 8 * c : 8 * c + 8, :], y.at[:, rows, c * 128 : (c + 1) * 128], sems.at[4 + c]
            ).start()

    for c in range(2):
        part = y.at[:, :, c * 128 : (c + 1) * 128]
        pltpu.make_async_copy(part, part, sems.at[4 + c]).wait()


def shards(
    ocean_state, canopy_type, drag_table, ocean_list, ice_list, weight_list, area_table, ice_temp, ice_cond, ice_vel
):
    st = ocean_state.reshape(FK, CJ, CI)
    olist, ilist, wlist = (x.reshape(DEV, SLOTS) for x in (ocean_list, ice_list, weight_list))
    itemp, icond = (x.reshape(64, 128) for x in (ice_temp, ice_cond))
    ivel = ice_vel.reshape(2, 64, 128).transpose(1, 0, 2).reshape(128, 128)
    area = area_table.reshape(1, 64)
    S = jax.ShapeDtypeStruct
    V = pltpu.VMEM
    out, tuv, rowlo, rowhi, colw, cole = pl.pallas_call(
        gather_kernel,
        out_shape=(
            S((DEV * ROWS, 128), f32), S((3 * 128, 128), f32), S((FK, CI), f32), S((FK, CI), f32),
            S((CJ, 128), f32), S((CJ, 128), f32),
        ),
        in_specs=[ANY] * 3 + [VM] * 7,
        out_specs=(VM,) * 6,
        scratch_shapes=[
            V((2, FK, CJ, 128), f32), V((768, 256), bf16), V((256, 256), bf16),
            V((128, 128), i32), V((128, 128), i32), V((3 * 128, 128), f32), V((4 * 128, 128), f32),
            pltpu.SMEM((128, 128), i32), pltpu.SMEM((128, 128), i32), pltpu.SemaphoreType.DMA((10,)),
        ],
        compiler_params=pltpu.CompilerParams(vmem_limit_bytes=LIMIT),
        name="gather_slots",
    )(st, olist, ilist, olist, ilist, wlist, area, itemp, icond, ivel)
    out3 = out.reshape(DEV, ROWS, 128)
    q, inb = pl.pallas_call(
        stencil_kernel,
        out_shape=(S((16, FK, 16, 128), f32), S((DEV, ROWS, 128), f32)),
        in_specs=[ANY] + [VM] * 7,
        out_specs=(VM, VM),
        scratch_shapes=[
            V((2, FK, 144, 128), f32), V((K, 8, 128), f32), V((DEV, ROWS, 128), f32),
            V((FK, CI), f32), V((FK, CI), f32), V((CJ, 128), f32), V((CJ, 128), f32),
            pltpu.SemaphoreType.DMA((4, 2)), pltpu.SemaphoreType.DMA((5,)),
            pltpu.SemaphoreType.DMA((5,)), pltpu.SemaphoreType.DMA((4,)),
        ],
        compiler_params=pltpu.CompilerParams(vmem_limit_bytes=LIMIT, collective_id=0, has_side_effects=True),
        name="exchange_stencil",
    )(st, out3, canopy_type, drag_table, rowlo, rowhi, colw, cole)
    y, itemp_next = pl.pallas_call(
        finish_kernel,
        out_shape=(S((FK, CJ, CI), f32), S((64, 128), f32)),
        in_specs=[ANY] * 3 + [VM] * 9,
        out_specs=(ANY, VM),
        scratch_shapes=[
            V((16, FK, 16, 128), f32), V((2, CJ, 128), f32), V((K, 8, 128), f32),
            V((128, 128), i32), V((128, 128), i32), V((4 * 128, 128), f32), V((128, 128), f32),
            V((4 * CJ, CI), f32), V((64, 128), f32), V((4 * CJ, 1024), bf16), V((CI, 512), bf16),
            pltpu.SMEM((128, 128), i32), pltpu.SMEM((128, 128), i32), pltpu.SemaphoreType.DMA((6,)),
        ],
        compiler_params=pltpu.CompilerParams(vmem_limit_bytes=LIMIT),
        name="scatter_solve",
    )(st, olist, ilist, q, inb.reshape(DEV * ROWS, 128), out, tuv, olist, ilist, canopy_type, drag_table, itemp)
    return y.reshape(ocean_state.shape), itemp_next.reshape(ice_temp.shape)


def solution(mesh):
    return jax.shard_map(
        shards,
        mesh=mesh,
        in_specs=(
            P(None, None, "lat", "lon"),
            P("lat", "lon"),
            P(),
            P(("lon", "lat"), None),
            P(("lon", "lat"), None),
            P(("lon", "lat"), None),
            P(),
            P(("lon", "lat"), None),
            P(("lon", "lat"), None),
            P(("lon", "lat"), None, None),
        ),
        out_specs=(P(None, None, "lat", "lon"), P(("lon", "lat"), None)),
        check_vma=False,
    )
```

time: 313 us -> 75.9 us (0.24); the launches traced: 307 us -> 75.7 us
  other arithmetic: 147 us -> 0 us
  Pallas kernels: 0 us -> 75 us
  matrix products: 60.8 us -> 0 us
  local copies, waits for them, and re-layouts: 60.1 us -> 0 us
  starting transfers between devices: 33.8 us -> 0 us
  waiting for transfers between devices: 3.56 us -> 0 us
    pallas_call x0 -> x3, Pallas kernels: none -> 75 us  [the longest x1 35.8 us: shards(): pl.pallas_call(stencil_kernel, out_shape=(S((16, FK, 16, 128), f32), S((D...]
    dot_general x5 -> x0, matrix products: 60.8 us -> none  [the longest x2 31.4 us: spread_slots(): lax.dot_general(weighted, low_hot, (((1,), (1,)), ((), ())), precision=la...]
    sub x3 -> x0, other arithmetic: 37.7 us -> none  [the longest x1 37.1 us: provisional(): laplace = east_side + west_side + north_side + south_side - 4.0 * centre]
    concatenate x3 -> x0, other arithmetic: 33.6 us -> none  [the longest x2 23.1 us: extended_2(): array = jnp.concatenate([before, array, after], axis=dim)]
    all_to_all x2 -> x0, starting transfers between devices: 19.1 us -> none  [the longest x1 9.82 us: shards(): lax.all_to_all(outgoing, ('lon', 'lat'), split_axis=1, concat_axis=1, til...]
    slice x10 -> x0, local copies, waits for them, and re-layouts: 18.3 us -> none  [the longest x4 12.4 us: extended_2(): last = lax.slice_in_dim(array, length - width, length, axis=dim)]
    unnamed x69 -> x0, local copies, waits for them, and re-layouts: 17.5 us -> none
    scatter x1 -> x0, local copies, waits for them, and re-layouts: 15.6 us -> none  [shards(): extended = extended.at[:, :, block_rows + 1, 1:-1].set(folded)]
  transfers between devices with their start and end apart: 10 -> 0, of which waited for: 1 -> 0; matrix products, arithmetic and copies ran while one was open for 62% -> 0% of each run, Pallas kernels for 0% -> 0%
where the time goes in v1:
time: 75.9 us; the launch traced here: 75.7 us
  Pallas kernels  75 us (99%)
    pallas_call x1, Pallas kernels, shards(): pl.pallas_call(stencil_kernel, out_shape=(S((16, FK, 16, 128), f32), S((D...  35.8 us
    pallas_call x1, Pallas kernels, shards(): pl.pallas_call(finish_kernel, out_shape=(S((FK, CJ, CI), f32), S((64, 128...  23 us
    pallas_call x1, Pallas kernels, shards(): pl.pallas_call(gather_kernel, out_shape=(S((DEV * ROWS, 128), f32), S((3...  16.3 us

profile of v1, /device:TPU:1, one launch (start us, length us, event | category | flops | bytes accessed | tf_op | source)
XLA Modules:
  0.0 75.7 jit_solution(2683227059363445882)
XLA Ops:
  0.6 16.3 %gather_slots.1 = (f32[1024,128]{1,0:T(8,128)}, f32[384,128]{1,0:T(8,128)}, f32[80,256]{1,0:T(8,128)}, f32[80,256]{1,0:T(8,128)}, f32[128,128]{1,0:T(8,128)}, /*index=5*/f32[128,128]{1,0:T(8,128)}) custom-call(f32[80,128,256]{2,1,0:T(8,128)} %bitcast.16, s32[128,128]{1,0:T(8,128)} %bitcast.20, s32[128,128]{1,0:T(8,128)} %bitcast.24, s32[128,128]{1,0:T(8,128)} %bitcast.21, ...), custom_call_target="tpu_custom_call" | custom-call | tf_op jit(solution)/shard_map/gather_slots/pallas_call | solution.py:551
  16.9 35.8 %exchange_stencil.1 = (f32[16,80,16,128]{3,2,1,0:T(8,128)}, f32[128,8,128]{2,1,0:T(8,128)}) custom-call(f32[80,128,256]{2,1,0:T(8,128)} %bitcast.17, f32[128,8,128]{2,1,0:T(8,128)} %bitcast.19, s32[128,256]{1,0:T(8,128)} %canopy.3, f32[8,20]{1,0:T(8,128)} %table.3, f32[80,256]{1,0:T(8,128)} %get-tuple-element.13.rowlo, f32[80,256]{1,0:T(8,128)} %get-tuple-element.14.rowhi, ...), custom_call_target="tpu_custom_call" | custom-call | tf_op jit(solution)/shard_map/exchange_stencil/pallas_call | solution.py:568
  52.7 23.0 %scatter_solve.1 = (f32[80,128,256]{2,1,0:T(8,128)}, f32[64,128]{1,0:T(8,128)}) custom-call(f32[80,128,256]{2,1,0:T(8,128)} %bitcast.18, s32[128,128]{1,0:T(8,128)} %bitcast.22, s32[128,128]{1,0:T(8,128)} %bitcast.26, f32[16,80,16,128]{3,2,1,0:T(8,128)} %get-tuple-element.17.q, f32[1024,128]{1,0:T(8,128)} %bitcast.28, f32[1024,128]{1,0:T(8,128)} %get-tuple-element.12.out, ...), custom_call_target="tpu_custom_call" | custom-call | tf_op jit(solution)/shard_map/scatter_solve/pallas_call | solution.py:582

commit v2 on v1

--- a/solution.py
+++ b/solution.py
@@ -82,27 +82,22 @@
 def gather_kernel(
     st, olist_any, ilist_any, olist, ilist, wlist, area, itemp, icond, ivel,
     out, tuv, rowlo, rowhi, colw, cole,
-    full, otab, itab, opack, ipack, ogot, igot, oflag, iflag, sems,
+    full, surf, otab, itab, opack, ipack, ogot, igot, oflag, iflag, sems,
 ):
     flags = [
         pltpu.make_async_copy(olist_any, oflag, sems.at[0]),
         pltpu.make_async_copy(ilist_any, iflag, sems.at[1]),
     ]
-    loads = []
-    for n, f in enumerate((0, 2, 3, 1)):
-        loads.append([
-            pltpu.make_async_copy(
-                st.at[f * K : (f + 1) * K, :, c * 128 : (c + 1) * 128],
-                full.at[c, f * K : (f + 1) * K],
-                sems.at[2 + 2 * n + c],
-            )
-            for c in range(2)
-        ])
-    for copy in flags:
+    tops = [
+        pltpu.make_async_copy(st.at[f * K, :, c * 128 : (c + 1) * 128], surf.at[n, c], sems.at[2])
+        for n, f in enumerate((0, 2, 3))
+        for c in range(2)
+    ]
+    state = [
+        pltpu.make_async_copy(st.at[:, :, c * 128 : (c + 1) * 128], full.at[c], sems.at[3 + c]) for c in range(2)
+    ]
+    for copy in tops + flags + state:
         copy.start()
-    for pair in loads:
-        for copy in pair:
-            copy.start()
     pack_list(olist, opack)
     pack_list(ilist, ipack)
     ogot[...] = jnp.zeros_like(ogot)
@@ -140,25 +135,41 @@
     for copy in flags:
         copy.wait()
 
-    @pl.loop(0, 32)
+    @pl.loop(0, 32, step=4)
     def _(t):
-        @pl.when(long_pairs(iflag, 4 * t, 4))
+        @pl.when(long_pairs(iflag, 4 * t, 16))
         def _():
-            gather(32 + t, ipack, itab, 4, 32, igot)
-
+            for j in range(4):
+                gather(32 + t + j, ipack, itab, 4, 32, igot)
+
+    pltpu.make_async_copy(surf, surf, sems.at[2]).wait()
     for n in range(3):
-        for copy in loads[n]:
-            copy.wait()
-    for n, f in enumerate((0, 2, 3)):
         for c in range(2):
-            high, low = split(full[c, f * K])
+            high, low = split(surf[n, c])
             otab[128 * n : 128 * n + 128, c * 128 : (c + 1) * 128] = high
             otab[384 + 128 * n : 512 + 128 * n, c * 128 : (c + 1) * 128] = low
-
-    @pl.loop(0, 32, step=2)
+    for copy in state:
+        copy.wait()
+
+    def columns(m):
+        lane = lanes()
+        rows = pl.ds(pl.multiple_of(8 * m, 8), 8)
+        west = jnp.zeros((8, 128), f32)
+        east = jnp.zeros((8, 128), f32)
+        for fk in range(FK):
+            both = jnp.where(lane == 127, full[1, fk, rows, :], full[0, fk, rows, :])
+            both = pltpu.roll(both, fk, 1) if fk else both
+            west = jnp.where(lane == fk, both, west)
+            east = jnp.where(lane == (fk - 1) % 128, both, east)
+        colw[rows, :] = west
+        cole[rows, :] = east
+
+    @pl.loop(0, 8)
     def _(t):
+        for j in range(4):
+            gather(4 * t + j, opack, otab, 3, 128, ogot)
         for j in range(2):
-            gather(t + j, opack, otab, 3, 128, ogot)
+            columns(2 * t + j)
 
     @pl.loop(0, 32)
     def _(t):
@@ -196,26 +207,10 @@
         for f in range(SENT, ROWS):
             out[pl.ds(64 * g + f, 8, stride=8), :] = jnp.zeros((8, 128), f32)
 
-    for copy in loads[3]:
-        copy.wait()
     for fk in range(FK):
         for c in range(2):
             rowlo[fk : fk + 1, c * 128 : (c + 1) * 128] = full[c, fk, 0:1, :]
             rowhi[fk : fk + 1, c * 128 : (c + 1) * 128] = full[c, fk, 127:128, :]
-
-    @pl.loop(0, 16)
-    def _(m):
-        lane = lanes()
-        rows = pl.ds(pl.multiple_of(8 * m, 8), 8)
-        west = jnp.zeros((8, 128), f32)
-        east = jnp.zeros((8, 128), f32)
-        for fk in range(FK):
-            both = jnp.where(lane == 127, full[1, fk, rows, :], full[0, fk, rows, :])
-            both = pltpu.roll(both, fk, 1) if fk else both
-            west = jnp.where(lane == fk, both, west)
-            east = jnp.where(lane == (fk - 1) % 128, both, east)
-        colw[rows, :] = west
-        cole[rows, :] = east
 
 
 def stencil_row(m, buf, q, canopy, east_col, west_col, drag, lat):
@@ -227,38 +222,35 @@
     kind = [canopy[rows, c * 128 : (c + 1) * 128] for c in range(2)]
     row = (lat * CJ + 8 * m + sub).astype(f32)
     cor = 4.0 * (2.0 * (row + 0.5) / (CJ * NLAT) - 1.0)
-    elim = [[None] * 2 for _ in range(NF)]
-    gx, gy = [None] * 2, [None] * 2
-    for k in range(K):
-        C, E, W, N, S = ([[None] * 2 for _ in range(NF)] for _ in range(5))
-        for f in range(NF):
-            fk = f * K + k
-            for c in range(2):
-                C[f][c] = buf[c, fk, pl.ds(pl.multiple_of(8 + 8 * m, 8), 8), :]
-                N[f][c] = buf[c, fk, pl.ds(9 + 8 * m, 8), :]
-                S[f][c] = buf[c, fk, pl.ds(7 + 8 * m, 8), :]
-            e0, e1 = (pltpu.roll(C[f][c], 127, 1) for c in range(2))
-            w0, w1 = (pltpu.roll(C[f][c], 1, 1) for c in range(2))
-            E[f][0] = jnp.where(last, e1, e0)
-            E[f][1] = jnp.where(last, pltpu.roll(east_halo, (127 - fk) % 128, 1), e1)
-            W[f][0] = jnp.where(first, pltpu.roll(west_halo, (1 - fk) % 128, 1), w0)
-            W[f][1] = jnp.where(first, w0, w1)
-        for c in range(2):
-            u, v = C[2][c], C[3][c]
-            eE = (0.4 - u) - E[2][c]
-            eW = (0.4 + u) + W[2][c]
-            eN = (0.4 - v) - N[3][c]
-            eS = (0.4 + v) + S[3][c]
+    for c in range(2):
+        elim = [None] * NF
+        gx = gy = None
+        for k in range(K):
+            C, E, W, N, S = ([None] * NF for _ in range(5))
+            for f in range(NF):
+                fk = f * K + k
+                mine, other = (buf[d, fk, pl.ds(pl.multiple_of(8 + 8 * m, 8), 8), :] for d in (c, 1 - c))
+                C[f] = mine
+                N[f] = buf[c, fk, pl.ds(9 + 8 * m, 8), :]
+                S[f] = buf[c, fk, pl.ds(7 + 8 * m, 8), :]
+                if c == 0:
+                    E[f] = pltpu.roll(jnp.where(first, other, mine), 127, 1)
+                    W[f] = jnp.where(first, pltpu.roll(west_halo, (1 - fk) % 128, 1), pltpu.roll(mine, 1, 1))
+                else:
+                    E[f] = jnp.where(last, pltpu.roll(east_halo, (127 - fk) % 128, 1), pltpu.roll(mine, 127, 1))
+                    W[f] = pltpu.roll(jnp.where(last, other, mine), 1, 1)
+            u, v = C[2], C[3]
+            eE = (0.4 - u) - E[2]
+            eW = (0.4 + u) + W[2]
+            eN = (0.4 - v) - N[3]
+            eS = (0.4 + v) + S[3]
             mid = 36.8 + ((eE + eW) + (eN + eS))
-            new = [
-                (C[f][c] * mid + E[f][c] * eE) + (W[f][c] * eW + N[f][c] * eN) + S[f][c] * eS
-                for f in range(NF)
-            ]
-            hx = 0.4 * (E[1][c] - W[1][c]) - 0.1 * (E[0][c] - W[0][c])
-            hy = 0.4 * (N[1][c] - S[1][c]) - 0.1 * (N[0][c] - S[0][c])
-            px = hx if k == 0 else gx[c] + hx
-            py = hy if k == 0 else gy[c] + hy
-            gx[c], gy[c] = px + hx, py + hy
+            new = [(C[f] * mid + E[f] * eE) + (W[f] * eW + N[f] * eN) + S[f] * eS for f in range(NF)]
+            hx = 0.4 * (E[1] - W[1]) - 0.1 * (E[0] - W[0])
+            hy = 0.4 * (N[1] - S[1]) - 0.1 * (N[0] - S[0])
+            px = hx if k == 0 else gx + hx
+            py = hy if k == 0 else gy + hy
+            gx, gy = px + hx, py + hy
             new[2] = new[2] + (cor * v - px)
             new[3] = new[3] - (cor * u + py)
             if k > 0:
@@ -267,8 +259,8 @@
                 new[2], new[3] = new[2] * damp, new[3] * damp
             for f in range(NF):
                 if k > 1:
-                    new[f] = new[f] + FWD[k] * elim[f][c]
-                elim[f][c] = new[f]
+                    new[f] = new[f] + FWD[k] * elim[f]
+                elim[f] = new[f]
                 q[m, f * K + k, c * 8 : (c + 1) * 8, :] = new[f]
 
 
@@ -279,8 +271,8 @@
 
 def stencil_kernel(
     st, out, canopy, table, rowlo, rowhi, colw, cole,
-    q, inb,
-    buf, drag, mid, north, south, east_col, west_col, sems, hops, halo_send, halo_recv,
+    q_any, inb,
+    buf, q, drag, mid, north, south, east_col, west_col, sems, hops, halo_send, halo_recv,
 ):
     lon, lat = lax.axis_index("lon"), lax.axis_index("lat")
     loads = [
@@ -388,8 +380,11 @@
 
         @pl.loop(0, 4)
         def _(j):
-            stencil_row(4 * g + j, buf, q, canopy, east_col, west_col, drag, lat)
-
+            m = 4 * g + j
+            stencil_row(m, buf, q, canopy, east_col, west_col, drag, lat)
+            pltpu.make_async_copy(q.at[m], q_any.at[m], hops.at[5]).start()
+
+    pltpu.make_async_copy(q, q_any, hops.at[5]).wait()
     some = inb.at[0 : (NLAT - 1) * NLON]
     pltpu.make_async_copy(some, some, hops.at[4]).wait()
     pltpu.make_async_copy(some, some, hops.at[3]).wait()
@@ -411,9 +406,9 @@
 
 
 def finish_kernel(
-    st, olist_any, ilist_any, q, inb, out, tuv, olist, ilist, canopy, table, itemp,
+    st, olist_any, ilist_any, q_any, inb, out, tuv, olist, ilist, canopy, table, itemp,
     y, itemp_next,
-    ybuf, salt, drag, opack, ipack, oval, ival, oacc, iacc, wide, cols, oflag, iflag, sems,
+    q, ybuf, salt, drag, opack, ipack, oval, ival, oacc, iacc, owide, ocols, iwide, icols, oflag, iflag, sems,
 ):
     flags = [
         pltpu.make_async_copy(olist_any, oflag, sems.at[0]),
@@ -423,7 +418,8 @@
         pltpu.make_async_copy(st.at[K, :, c * 128 : (c + 1) * 128], salt.at[c], sems.at[2 + c])
         for c in range(2)
     ]
-    for copy in flags + salts:
+    state = pltpu.make_async_copy(q_any, q, sems.at[6])
+    for copy in flags + salts + [state]:
         copy.start()
     drag_levels(table, drag)
     pack_list(olist, opack)
@@ -450,36 +446,41 @@
     oacc[...] = jnp.zeros_like(oacc)
     iacc[...] = jnp.zeros_like(iacc)
 
-    def scatter(tile, packed, values, fields, rows, width, acc):
+    def hot_columns(tile, packed, width, cols):
         for h in range(4):
-            index = packed[pl.ds(4 * tile + h, 1), :]
-            here = slice(128 * h, 128 * h + 128)
-            cols[0:width, here] = jnp.where(one_hot(index & (width - 1), width), 1.0, 0.0).astype(bf16)
-            mask = one_hot(index >> (width.bit_length() - 1), rows)
-            for f in range(fields):
-                value = values[pl.ds(128 * f + 4 * tile + h, 1), :]
+            index = packed[pl.ds(4 * tile + h, 1), :] & (width - 1)
+            cols[:, 128 * h : 128 * h + 128] = jnp.where(one_hot(index, width), 1.0, 0.0).astype(bf16)
+
+    def add(wide, cols, acc):
+        acc[...] += lax.dot_general(wide, cols, (((1,), (1,)), ((), ())), preferred_element_type=f32)
+
+    def scatter_ocean(tile):
+        hot_columns(tile, opack, CI, ocols)
+        for h in range(4):
+            mask = one_hot(opack[pl.ds(4 * tile + h, 1), :] >> 8, CJ)
+            for f in range(4):
+                value = oval[pl.ds(128 * f + 4 * tile + h, 1), :]
                 high = value.astype(bf16).astype(f32)
                 for n, part in enumerate((high, value - high)):
-                    part = jnp.where(mask, jnp.broadcast_to(part, (rows, 128)), 0.0).astype(bf16)
-                    wide[rows * f : rows * (f + 1), 512 * n + 128 * h : 512 * n + 128 * h + 128] = part
-        hot = cols[0:width, :]
-        both = jnp.concatenate([hot, hot], axis=1)
-        acc[...] += lax.dot_general(
-            wide[0 : rows * fields, :], both, (((1,), (1,)), ((), ())), preferred_element_type=f32
-        )
-
-    def scatter_ocean(tile):
-        scatter(tile, opack, oval, 4, CJ, CI, oacc)
+                    part = jnp.where(mask, jnp.broadcast_to(part, (CJ, 128)), 0.0).astype(bf16)
+                    owide[CJ * f : CJ * (f + 1), 512 * n + 128 * h : 512 * n + 128 * h + 128] = part
+        hot = ocols[...]
+        add(owide[...], jnp.concatenate([hot, hot], axis=1), oacc)
 
     def scatter_ice(tile):
-        scatter(tile, ipack, ival, 1, 64, 128, iacc)
+        hot_columns(tile, ipack, 128, icols)
+        for h in range(4):
+            mask = one_hot(ipack[pl.ds(4 * tile + h, 1), :] >> 7, 64)
+            value = ival[pl.ds(4 * tile + h, 1), :]
+            high = value.astype(bf16).astype(f32)
+            for n, part in enumerate((high, value - high)):
+                part = jnp.where(mask, jnp.broadcast_to(part, (64, 128)), 0.0).astype(bf16)
+                iwide[64 * n : 64 * n + 64, 128 * h : 128 * h + 128] = part
+        add(iwide[...], icols[...], iacc)
 
     @pl.loop(0, 16)
     def _(t):
         scatter_ocean(t)
-
-    @pl.loop(0, 16)
-    def _(t):
         scatter_ice(t)
 
     for copy in flags:
@@ -495,8 +496,8 @@
         def _():
             scatter_ice(16 + t)
 
-    itemp_next[...] = itemp[...] - 0.25 * iacc[...]
-    for copy in salts:
+    itemp_next[...] = itemp[...] - 0.25 * (iacc[0:64, :] + iacc[64:128, :])
+    for copy in salts + [state]:
         copy.wait()
 
     @pl.loop(0, 16)
@@ -557,9 +558,9 @@
         in_specs=[ANY] * 3 + [VM] * 7,
         out_specs=(VM,) * 6,
         scratch_shapes=[
-            V((2, FK, CJ, 128), f32), V((768, 256), bf16), V((256, 256), bf16),
+            V((2, FK, CJ, 128), f32), V((3, 2, CJ, 128), f32), V((768, 256), bf16), V((256, 256), bf16),
             V((128, 128), i32), V((128, 128), i32), V((3 * 128, 128), f32), V((4 * 128, 128), f32),
-            pltpu.SMEM((128, 128), i32), pltpu.SMEM((128, 128), i32), pltpu.SemaphoreType.DMA((10,)),
+            pltpu.SMEM((128, 128), i32), pltpu.SMEM((128, 128), i32), pltpu.SemaphoreType.DMA((5,)),
         ],
         compiler_params=pltpu.CompilerParams(vmem_limit_bytes=LIMIT),
         name="gather_slots",
@@ -568,12 +569,12 @@
     q, inb = pl.pallas_call(
         stencil_kernel,
         out_shape=(S((16, FK, 16, 128), f32), S((DEV, ROWS, 128), f32)),
-        in_specs=[ANY] + [VM] * 7,
-        out_specs=(VM, VM),
+        in_specs=[ANY, ANY, VM, VM] + [ANY] * 4,
+        out_specs=(ANY, ANY),
         scratch_shapes=[
-            V((2, FK, 144, 128), f32), V((K, 8, 128), f32), V((DEV, ROWS, 128), f32),
+            V((2, FK, 144, 128), f32), V((16, FK, 16, 128), f32), V((K, 8, 128), f32), V((DEV, ROWS, 128), f32),
             V((FK, CI), f32), V((FK, CI), f32), V((CJ, 128), f32), V((CJ, 128), f32),
-            pltpu.SemaphoreType.DMA((4, 2)), pltpu.SemaphoreType.DMA((5,)),
+            pltpu.SemaphoreType.DMA((4, 2)), pltpu.SemaphoreType.DMA((6,)),
             pltpu.SemaphoreType.DMA((5,)), pltpu.SemaphoreType.DMA((4,)),
         ],
         compiler_params=pltpu.CompilerParams(vmem_limit_bytes=LIMIT, collective_id=0, has_side_effects=True),
@@ -582,13 +583,14 @@
     y, itemp_next = pl.pallas_call(
         finish_kernel,
         out_shape=(S((FK, CJ, CI), f32), S((64, 128), f32)),
-        in_specs=[ANY] * 3 + [VM] * 9,
+        in_specs=[ANY] * 4 + [VM] * 8,
         out_specs=(ANY, VM),
         scratch_shapes=[
-            V((16, FK, 16, 128), f32), V((2, CJ, 128), f32), V((K, 8, 128), f32),
+            V((16, FK, 16, 128), f32), V((16, FK, 16, 128), f32), V((2, CJ, 128), f32), V((K, 8, 128), f32),
             V((128, 128), i32), V((128, 128), i32), V((4 * 128, 128), f32), V((128, 128), f32),
-            V((4 * CJ, CI), f32), V((64, 128), f32), V((4 * CJ, 1024), bf16), V((CI, 512), bf16),
-            pltpu.SMEM((128, 128), i32), pltpu.SMEM((128, 128), i32), pltpu.SemaphoreType.DMA((6,)),
+            V((4 * CJ, CI), f32), V((128, 128), f32), V((4 * CJ, 1024), bf16), V((CI, 512), bf16),
+            V((128, 512), bf16), V((128, 512), bf16),
+            pltpu.SMEM((128, 128), i32), pltpu.SMEM((128, 128), i32), pltpu.SemaphoreType.DMA((7,)),
         ],
         compiler_params=pltpu.CompilerParams(vmem_limit_bytes=LIMIT),
         name="scatter_solve",

time: 75.9 us -> 62 us (0.82)
  the two profiles are of different devices: /device:TPU:1 before, /device:TPU:33 now
where the time goes in v2:
time: 62 us; the launch traced here: 61.7 us
  Pallas kernels  61.1 us (99%)
  between operations  0.65 us (1%)
    pallas_call x1, Pallas kernels, shards(): pl.pallas_call(stencil_kernel, out_shape=(S((16, FK, 16, 128), f32), S((D...  26 us
    pallas_call x1, Pallas kernels, shards(): pl.pallas_call(finish_kernel, out_shape=(S((FK, CJ, CI), f32), S((64, 128...  21 us
    pallas_call x1, Pallas kernels, shards(): pl.pallas_call(gather_kernel, out_shape=(S((DEV * ROWS, 128), f32), S((3...  14.1 us

profile of v2, /device:TPU:33, one launch (start us, length us, event | category | flops | bytes accessed | tf_op | source)
XLA Modules:
  0.0 61.7 jit_solution(12296069624905972346)
XLA Ops:
  0.6 14.1 %gather_slots.1 = (f32[1024,128]{1,0:T(8,128)}, f32[384,128]{1,0:T(8,128)}, f32[80,256]{1,0:T(8,128)}, f32[80,256]{1,0:T(8,128)}, f32[128,128]{1,0:T(8,128)}, /*index=5*/f32[128,128]{1,0:T(8,128)}) custom-call(f32[80,128,256]{2,1,0:T(8,128)} %bitcast.16, s32[128,128]{1,0:T(8,128)} %bitcast.20, s32[128,128]{1,0:T(8,128)} %bitcast.24, s32[128,128]{1,0:T(8,128)} %bitcast.21, ...), custom_call_target="tpu_custom_call" | custom-call | tf_op jit(solution)/shard_map/gather_slots/pallas_call | solution.py:552
  14.7 26.0 %exchange_stencil.1 = (f32[16,80,16,128]{3,2,1,0:T(8,128)}, f32[128,8,128]{2,1,0:T(8,128)}) custom-call(f32[80,128,256]{2,1,0:T(8,128)} %bitcast.17, f32[128,8,128]{2,1,0:T(8,128)} %bitcast.19, s32[128,256]{1,0:T(8,128)} %canopy.3, f32[8,20]{1,0:T(8,128)} %table.3, f32[80,256]{1,0:T(8,128)} %get-tuple-element.13.rowlo, f32[80,256]{1,0:T(8,128)} %get-tuple-element.14.rowhi, ...), custom_call_target="tpu_custom_call" | custom-call | tf_op jit(solution)/shard_map/exchange_stencil/pallas_call | solution.py:569
  40.7 21.0 %scatter_solve.1 = (f32[80,128,256]{2,1,0:T(8,128)}, f32[64,128]{1,0:T(8,128)}) custom-call(f32[80,128,256]{2,1,0:T(8,128)} %bitcast.18, s32[128,128]{1,0:T(8,128)} %bitcast.22, s32[128,128]{1,0:T(8,128)} %bitcast.26, f32[16,80,16,128]{3,2,1,0:T(8,128)} %get-tuple-element.17.q_any, f32[1024,128]{1,0:T(8,128)} %bitcast.28, ...), custom_call_target="tpu_custom_call" | custom-call | tf_op jit(solution)/shard_map/scatter_solve/pallas_call | solution.py:583

commit v3 on v2

--- a/solution.py
+++ b/solution.py
@@ -79,77 +79,56 @@
     return most >= 0
 
 
+def gather(tile, packed, table, fields, rows, got):
+    hots, his = [], []
+    for h in range(2):
+        row = packed[pl.ds(2 * tile + h, 1), :]
+        his.append(row >> 8)
+        hots.append(jnp.where(one_hot(row & 255, 256), 1.0, 0.0).astype(bf16))
+    res = jnp.dot(table[...], jnp.concatenate(hots, axis=1), preferred_element_type=f32)
+    half = fields * rows
+    res = res[:half] + res[half:]
+    for h in range(2):
+        mask = one_hot(his[h], rows)
+        for f in range(fields):
+            value = jnp.where(mask, res[f * rows : (f + 1) * rows, h * 128 : (h + 1) * 128], 0.0)
+            got[pl.ds(f * 128 + 2 * tile + h, 1), :] = jnp.sum(value, axis=0, keepdims=True)
+
+
+def unpack(got, f, g):
+    left = lanes() < 64
+    first = got[f * 128 + 8 * g : f * 128 + 8 * g + 8, :]
+    second = got[f * 128 + 64 + 8 * g : f * 128 + 72 + 8 * g, :]
+    return (
+        jnp.where(left, first, pltpu.roll(second, 64, 1)),
+        jnp.where(left, pltpu.roll(first, 64, 1), second),
+    )
+
+
 def gather_kernel(
-    st, olist_any, ilist_any, olist, ilist, wlist, area, itemp, icond, ivel,
-    out, tuv, rowlo, rowhi, colw, cole,
-    full, surf, otab, itab, opack, ipack, ogot, igot, oflag, iflag, sems,
+    st, olist_any, olist,
+    tuv, rowlo, rowhi, colw, cole,
+    full, surf, otab, opack, ogot, oflag, sems,
 ):
-    flags = [
-        pltpu.make_async_copy(olist_any, oflag, sems.at[0]),
-        pltpu.make_async_copy(ilist_any, iflag, sems.at[1]),
-    ]
+    flags = pltpu.make_async_copy(olist_any, oflag, sems.at[0])
     tops = [
-        pltpu.make_async_copy(st.at[f * K, :, c * 128 : (c + 1) * 128], surf.at[n, c], sems.at[2])
+        pltpu.make_async_copy(st.at[f * K, :, c * 128 : (c + 1) * 128], surf.at[n, c], sems.at[1])
         for n, f in enumerate((0, 2, 3))
         for c in range(2)
     ]
     state = [
-        pltpu.make_async_copy(st.at[:, :, c * 128 : (c + 1) * 128], full.at[c], sems.at[3 + c]) for c in range(2)
+        pltpu.make_async_copy(st.at[:, :, c * 128 : (c + 1) * 128], full.at[c], sems.at[2 + c]) for c in range(2)
     ]
-    for copy in tops + flags + state:
+    for copy in tops + [flags] + state:
         copy.start()
     pack_list(olist, opack)
-    pack_list(ilist, ipack)
     ogot[...] = jnp.zeros_like(ogot)
-    igot[...] = jnp.zeros_like(igot)
-    for f in range(4):
-        for c in range(2):
-            if f < 2:
-                x = (icond, itemp)[f][pl.ds(c, 32, stride=2), :]
-            else:
-                x = ivel[pl.ds(2 * c + f - 2, 32, stride=4), :]
-            high, low = split(x)
-            itab[32 * f : 32 * f + 32, c * 128 : (c + 1) * 128] = high
-            itab[128 + 32 * f : 160 + 32 * f, c * 128 : (c + 1) * 128] = low
-
-    def gather(tile, packed, table, fields, rows, got):
-        hots, his = [], []
-        for h in range(2):
-            row = packed[pl.ds(2 * tile + h, 1), :]
-            his.append(row >> 8)
-            hots.append(jnp.where(one_hot(row & 255, 256), 1.0, 0.0).astype(bf16))
-        res = jnp.dot(table[...], jnp.concatenate(hots, axis=1), preferred_element_type=f32)
-        half = fields * rows
-        res = res[:half] + res[half:]
-        for h in range(2):
-            mask = one_hot(his[h], rows)
-            for f in range(fields):
-                value = jnp.where(mask, res[f * rows : (f + 1) * rows, h * 128 : (h + 1) * 128], 0.0)
-                got[pl.ds(f * 128 + 2 * tile + h, 1), :] = jnp.sum(value, axis=0, keepdims=True)
-
-    @pl.loop(0, 32, step=4)
-    def _(t):
-        for j in range(4):
-            gather(t + j, ipack, itab, 4, 32, igot)
-
-    for copy in flags:
-        copy.wait()
-
-    @pl.loop(0, 32, step=4)
-    def _(t):
-        @pl.when(long_pairs(iflag, 4 * t, 16))
-        def _():
-            for j in range(4):
-                gather(32 + t + j, ipack, itab, 4, 32, igot)
-
-    pltpu.make_async_copy(surf, surf, sems.at[2]).wait()
+    pltpu.make_async_copy(surf, surf, sems.at[1]).wait()
     for n in range(3):
         for c in range(2):
             high, low = split(surf[n, c])
             otab[128 * n : 128 * n + 128, c * 128 : (c + 1) * 128] = high
             otab[384 + 128 * n : 512 + 128 * n, c * 128 : (c + 1) * 128] = low
-    for copy in state:
-        copy.wait()
 
     def columns(m):
         lane = lanes()
@@ -164,12 +143,22 @@
         colw[rows, :] = west
         cole[rows, :] = east
 
-    @pl.loop(0, 8)
+    @pl.loop(0, 4)
     def _(t):
         for j in range(4):
             gather(4 * t + j, opack, otab, 3, 128, ogot)
-        for j in range(2):
-            columns(2 * t + j)
+
+    for copy in state:
+        copy.wait()
+
+    @pl.loop(4, 8)
+    def _(t):
+        for j in range(4):
+            gather(4 * t + j, opack, otab, 3, 128, ogot)
+        for j in range(4):
+            columns(4 * (t - 4) + j)
+
+    flags.wait()
 
     @pl.loop(0, 32)
     def _(t):
@@ -177,36 +166,11 @@
         def _():
             gather(32 + t, opack, otab, 3, 128, ogot)
 
-    left = lanes() < 64
-
-    def unpack(got, f, g):
-        first = got[f * 128 + 8 * g : f * 128 + 8 * g + 8, :]
-        second = got[f * 128 + 64 + 8 * g : f * 128 + 72 + 8 * g, :]
-        return (
-            jnp.where(left, first, pltpu.roll(second, 64, 1)),
-            jnp.where(left, pltpu.roll(first, 64, 1), second),
-        )
-
-    areas = jnp.broadcast_to(jnp.concatenate([area[...], area[...]], axis=1), (8, 128))
     for g in range(8):
         for n in range(3):
             even, odd = unpack(ogot, n, g)
             tuv[pl.ds(128 * n + 16 * g, 8, stride=2), :] = even
             tuv[pl.ds(128 * n + 16 * g + 1, 8, stride=2), :] = odd
-            if n == 0:
-                out[pl.ds(128 * g, 8, stride=16), :] = even
-                out[pl.ds(128 * g + 8, 8, stride=16), :] = odd
-        for f in range(4):
-            even, odd = unpack(igot, f, g)
-            out[pl.ds(128 * g + 2 + f, 8, stride=16), :] = even
-            out[pl.ds(128 * g + 10 + f, 8, stride=16), :] = odd
-    for g in range(16):
-        index = wlist[8 * g : 8 * g + 8, :]
-        value = jnp.where(index >= 0, take(areas, index & 63, 1), 0.0)
-        out[pl.ds(64 * g + 1, 8, stride=8), :] = value
-        for f in range(SENT, ROWS):
-            out[pl.ds(64 * g + f, 8, stride=8), :] = jnp.zeros((8, 128), f32)
-
     for fk in range(FK):
         for c in range(2):
             rowlo[fk : fk + 1, c * 128 : (c + 1) * 128] = full[c, fk, 0:1, :]
@@ -269,10 +233,30 @@
         drag[k] = jnp.broadcast_to(table[:, k : k + 1] * (0.1 / SCALE), (8, 128))
 
 
+def ice_messages(ilist, wlist, area, itemp, icond, ivel, msg, itab, ipack, igot):
+    @pl.loop(0, 64, step=4)
+    def _(t):
+        for j in range(4):
+            gather(t + j, ipack, itab, 4, 32, igot)
+
+    areas = jnp.broadcast_to(jnp.concatenate([area[...], area[...]], axis=1), (8, 128))
+    for g in range(8):
+        for f in range(4):
+            even, odd = unpack(igot, f, g)
+            msg[pl.ds(128 * g + 2 + f, 8, stride=16), :] = even
+            msg[pl.ds(128 * g + 10 + f, 8, stride=16), :] = odd
+    for g in range(16):
+        index = wlist[8 * g : 8 * g + 8, :]
+        value = jnp.where(index >= 0, take(areas, index & 63, 1), 0.0)
+        msg[pl.ds(64 * g + 1, 8, stride=8), :] = value
+        for f in range(SENT, ROWS):
+            msg[pl.ds(64 * g + f, 8, stride=8), :] = jnp.zeros((8, 128), f32)
+
+
 def stencil_kernel(
-    st, out, canopy, table, rowlo, rowhi, colw, cole,
-    q_any, inb,
-    buf, q, drag, mid, north, south, east_col, west_col, sems, hops, halo_send, halo_recv,
+    st, tuv, ilist, wlist, area, itemp, icond, ivel, canopy, table, rowlo, rowhi, colw, cole,
+    q_any, inb, out,
+    buf, q, drag, msg, temps, itab, ipack, igot, mid_a, mid_b, north, south, east_col, west_col, sems, hops, halo_send, halo_recv,
 ):
     lon, lat = lax.axis_index("lon"), lax.axis_index("lat")
     loads = [
@@ -290,11 +274,23 @@
         for copy in pair:
             copy.start()
 
+    surface = pltpu.make_async_copy(tuv.at[0:128], temps, hops.at[13])
+    surface.start()
     barrier = pltpu.get_barrier_semaphore()
     for i in range(1, NLON):
         pl.semaphore_signal(barrier, inc=1, device_id=(lax.rem(lon + i, NLON), lat), device_id_type=MESH)
     for i in range(1, NLAT):
         pl.semaphore_signal(barrier, inc=1, device_id=(lon, lax.rem(lat + i, NLAT)), device_id_type=MESH)
+    pack_list(ilist, ipack)
+    for f in range(4):
+        for c in range(2):
+            if f < 2:
+                x = (icond, itemp)[f][pl.ds(c, 32, stride=2), :]
+            else:
+                x = ivel[pl.ds(2 * c + f - 2, 32, stride=4), :]
+            high, low = split(x)
+            itab[32 * f : 32 * f + 32, c * 128 : (c + 1) * 128] = high
+            itab[128 + 32 * f : 160 + 32 * f, c * 128 : (c + 1) * 128] = low
     pl.semaphore_wait(barrier, NLON + NLAT - 2)
 
     def halo(src, dst, n, target):
@@ -323,14 +319,52 @@
             device_id=(NLON - 1 - lon, lat), device_id_type=MESH,
         ).start()
 
+    def hop(src, dst, n, target):
+        return pltpu.make_async_remote_copy(
+            src_ref=src, dst_ref=dst, send_sem=hops.at[n], recv_sem=hops.at[n + 1],
+            device_id=target, device_id_type=MESH,
+        )
+
+    ice_messages(ilist, wlist, area, itemp, icond, ivel, msg, itab, ipack, igot)
+    surface.wait()
+    for g in range(16):
+        msg[pl.ds(64 * g, 8, stride=8), :] = temps[8 * g : 8 * g + 8, :]
+    keep = pltpu.make_async_copy(msg, out, hops.at[12])
+    keep.start()
+    even = lax.rem(lon + lat, 2) == 0
+    by_a = msg.reshape(NLON, NLAT // 2, 2, ROWS, 128)
+    by_b = msg.reshape(NLON // 2, 2, NLAT, ROWS, 128)
+
+    def first_a(peer):
+        return by_a.at[peer, :, lax.rem(peer, 2), 0:SENT], mid_a.at[lon, :, 0:SENT]
+
+    def first_b(peer):
+        return by_b.at[:, 1 - lax.rem(peer, 2), peer, 0:SENT], mid_b.at[lat, :, 0:SENT]
+
     for i in range(1, NLON):
         peer = lax.rem(lon + i, NLON)
-        pltpu.make_async_remote_copy(
-            src_ref=out.at[pl.ds(peer * NLAT, NLAT)], dst_ref=mid.at[pl.ds(lon * NLAT, NLAT)],
-            send_sem=hops.at[0], recv_sem=hops.at[1], device_id=(peer, lat), device_id_type=MESH,
-        ).start()
-    own = pltpu.make_async_copy(out.at[pl.ds(lon * NLAT, NLAT)], mid.at[pl.ds(lon * NLAT, NLAT)], hops.at[2])
-    own.start()
+        hop(*first_a(peer), 0, (peer, lat)).start()
+    for i in range(1, NLAT):
+        peer = lax.rem(lat + i, NLAT)
+        hop(*first_b(peer), 2, (lon, peer)).start()
+    own_a = pltpu.make_async_copy(*first_a(lon), hops.at[8])
+    own_b = pltpu.make_async_copy(*first_b(lat), hops.at[9])
+    own_a.start()
+    own_b.start()
+    in4 = inb.reshape(NLON, NLAT, ROWS, 128)
+
+    def second_a(peer):
+        return mid_a.at[:, peer // 2, 0:SENT], in4.at[:, lat, 0:SENT]
+
+    def second_b(peer):
+        return mid_b.at[:, peer // 2, 0:SENT], in4.at[lon, :, 0:SENT]
+
+    def blocks(ref, n):
+        part = ref.at[0:n, 0:SENT]
+        return part, part
+
+    def taken(n, sem):
+        pltpu.make_async_copy(*blocks(inb, n), hops.at[sem]).wait()
 
     drag_levels(table, drag)
     to_west.wait_recv()
@@ -354,44 +388,66 @@
     for copy in loads[0]:
         copy.wait()
 
-    @pl.loop(0, 4)
+    @pl.loop(0, 8)
     def _(g):
-        @pl.when(g < 3)
+        @pl.when(lax.rem(g, 2) - jnp.where(g > 5, 1, 0) == 1)
         def _():
             for c in range(2):
                 pltpu.make_async_copy(
-                    st.at[:, 0:32, 0:128], buf.at[c, :, 8:40, :], sems.at[g + 1, c]
+                    st.at[:, 0:32, 0:128], buf.at[c, :, 8:40, :], sems.at[g // 2 + 1, c]
                 ).wait()
 
-        @pl.when(g == 2)
+        @pl.when(g == 3)
         def _():
-            many = mid.at[0 : (NLON - 1) * NLAT]
-            pltpu.make_async_copy(many, many, hops.at[1]).wait()
-            own.wait()
-            mid4 = mid.reshape(NLON, NLAT, ROWS, 128)
-            in4 = inb.reshape(NLON, NLAT, ROWS, 128)
-            for i in range(1, NLAT):
-                peer = lax.rem(lat + i, NLAT)
-                pltpu.make_async_remote_copy(
-                    src_ref=mid4.at[:, peer], dst_ref=in4.at[:, lat],
-                    send_sem=hops.at[3], recv_sem=hops.at[4], device_id=(lon, peer), device_id_type=MESH,
-                ).start()
-            pltpu.make_async_copy(mid4.at[:, lat], in4.at[:, lat], hops.at[2]).start()
-
-        @pl.loop(0, 4)
+            taken((NLON - 1) * NLAT // 2, 1)
+            taken((NLAT - 1) * NLON // 2, 3)
+            own_a.wait()
+            own_b.wait()
+
+            @pl.when(even)
+            def _():
+                pltpu.make_async_copy(*second_a(lat), hops.at[10]).start()
+                for i in range(2, NLAT, 2):
+                    peer = lax.rem(lat + i, NLAT)
+                    hop(*second_a(peer), 4, (lon, peer)).start()
+                for i in range(1, NLON, 2):
+                    peer = lax.rem(lon + i, NLON)
+                    hop(*second_b(peer), 6, (peer, lat)).start()
+
+            @pl.when(jnp.logical_not(even))
+            def _():
+                pltpu.make_async_copy(*second_b(lon), hops.at[11]).start()
+                for i in range(1, NLAT, 2):
+                    peer = lax.rem(lat + i, NLAT)
+                    hop(*second_a(peer), 4, (lon, peer)).start()
+                for i in range(2, NLON, 2):
+                    peer = lax.rem(lon + i, NLON)
+                    hop(*second_b(peer), 6, (peer, lat)).start()
+
+        @pl.loop(0, 2)
         def _(j):
-            m = 4 * g + j
+            m = 2 * g + j
             stencil_row(m, buf, q, canopy, east_col, west_col, drag, lat)
-            pltpu.make_async_copy(q.at[m], q_any.at[m], hops.at[5]).start()
-
-    pltpu.make_async_copy(q, q_any, hops.at[5]).wait()
-    some = inb.at[0 : (NLAT - 1) * NLON]
-    pltpu.make_async_copy(some, some, hops.at[4]).wait()
-    pltpu.make_async_copy(some, some, hops.at[3]).wait()
-    one = inb.at[0:NLON]
-    pltpu.make_async_copy(one, one, hops.at[2]).wait()
-    many = mid.at[0 : (NLON - 1) * NLAT]
-    pltpu.make_async_copy(many, many, hops.at[0]).wait()
+            pltpu.make_async_copy(q.at[m], q_any.at[m], hops.at[14]).start()
+
+    pltpu.make_async_copy(q, q_any, hops.at[14]).wait()
+    keep.wait()
+    @pl.when(even)
+    def _():
+        taken((NLAT - 1) * NLON, 5)
+        taken(NLON, 10)
+        taken((NLAT // 2 - 1) * NLON, 4)
+        taken((NLON // 2) * NLAT, 6)
+
+    @pl.when(jnp.logical_not(even))
+    def _():
+        taken((NLON - 1) * NLAT, 7)
+        taken(NLAT, 11)
+        taken((NLAT // 2) * NLON, 4)
+        taken((NLON // 2 - 1) * NLAT, 6)
+
+    taken((NLON - 1) * NLAT // 2, 0)
+    taken((NLAT - 1) * NLON // 2, 2)
     to_west.wait_send()
     to_east.wait_send()
     to_north.wait_send()
@@ -454,8 +510,8 @@
     def add(wide, cols, acc):
         acc[...] += lax.dot_general(wide, cols, (((1,), (1,)), ((), ())), preferred_element_type=f32)
 
-    def scatter_ocean(tile):
-        hot_columns(tile, opack, CI, ocols)
+    def scatter_ocean(tile, p=0):
+        hot_columns(tile, opack, CI, ocols.at[p])
         for h in range(4):
             mask = one_hot(opack[pl.ds(4 * tile + h, 1), :] >> 8, CJ)
             for f in range(4):
@@ -463,9 +519,8 @@
                 high = value.astype(bf16).astype(f32)
                 for n, part in enumerate((high, value - high)):
                     part = jnp.where(mask, jnp.broadcast_to(part, (CJ, 128)), 0.0).astype(bf16)
-                    owide[CJ * f : CJ * (f + 1), 512 * n + 128 * h : 512 * n + 128 * h + 128] = part
-        hot = ocols[...]
-        add(owide[...], jnp.concatenate([hot, hot], axis=1), oacc)
+                    owide[p, 512 * n + CJ * f : 512 * n + CJ * (f + 1), 128 * h : 128 * h + 128] = part
+        add(owide[p], ocols[p], oacc)
 
     def scatter_ice(tile):
         hot_columns(tile, ipack, 128, icols)
@@ -478,10 +533,12 @@
                 iwide[64 * n : 64 * n + 64, 128 * h : 128 * h + 128] = part
         add(iwide[...], icols[...], iacc)
 
-    @pl.loop(0, 16)
+    @pl.loop(0, 16, step=2)
     def _(t):
         scatter_ocean(t)
+        scatter_ocean(t + 1, 1)
         scatter_ice(t)
+        scatter_ice(t + 1)
 
     for copy in flags:
         copy.wait()
@@ -506,9 +563,10 @@
         sides = []
         for c in range(2):
             here = slice(8 * c, 8 * c + 8)
-            flux = [
-                oacc[pl.ds(pl.multiple_of(CJ * f + 8 * m, 8), 8), c * 128 : (c + 1) * 128] for f in range(4)
-            ]
+            flux = []
+            for f in range(4):
+                high, low = (pl.ds(pl.multiple_of(part + CJ * f + 8 * m, 8), 8) for part in (0, 4 * CJ))
+                flux.append(oacc[high, c * 128 : (c + 1) * 128] + oacc[low, c * 128 : (c + 1) * 128])
             top = [q[m, f * K, here, :] for f in range(4)]
             top[0] = top[0] + 20.0 * flux[0]
             top[1] = top[1] - 10.0 * (salt[c, rows, :] * flux[1])
@@ -549,37 +607,36 @@
     area = area_table.reshape(1, 64)
     S = jax.ShapeDtypeStruct
     V = pltpu.VMEM
-    out, tuv, rowlo, rowhi, colw, cole = pl.pallas_call(
+    tuv, rowlo, rowhi, colw, cole = pl.pallas_call(
         gather_kernel,
         out_shape=(
-            S((DEV * ROWS, 128), f32), S((3 * 128, 128), f32), S((FK, CI), f32), S((FK, CI), f32),
-            S((CJ, 128), f32), S((CJ, 128), f32),
+            S((3 * 128, 128), f32), S((FK, CI), f32), S((FK, CI), f32), S((CJ, 128), f32), S((CJ, 128), f32),
         ),
-        in_specs=[ANY] * 3 + [VM] * 7,
-        out_specs=(VM,) * 6,
+        in_specs=[ANY] * 2 + [VM],
+        out_specs=(VM,) * 5,
         scratch_shapes=[
-            V((2, FK, CJ, 128), f32), V((3, 2, CJ, 128), f32), V((768, 256), bf16), V((256, 256), bf16),
-            V((128, 128), i32), V((128, 128), i32), V((3 * 128, 128), f32), V((4 * 128, 128), f32),
-            pltpu.SMEM((128, 128), i32), pltpu.SMEM((128, 128), i32), pltpu.SemaphoreType.DMA((5,)),
+            V((2, FK, CJ, 128), f32), V((3, 2, CJ, 128), f32), V((768, 256), bf16), V((128, 128), i32),
+            V((3 * 128, 128), f32), pltpu.SMEM((128, 128), i32), pltpu.SemaphoreType.DMA((4,)),
         ],
         compiler_params=pltpu.CompilerParams(vmem_limit_bytes=LIMIT),
         name="gather_slots",
-    )(st, olist, ilist, olist, ilist, wlist, area, itemp, icond, ivel)
-    out3 = out.reshape(DEV, ROWS, 128)
-    q, inb = pl.pallas_call(
+    )(st, olist, olist)
+    q, inb, out = pl.pallas_call(
         stencil_kernel,
-        out_shape=(S((16, FK, 16, 128), f32), S((DEV, ROWS, 128), f32)),
-        in_specs=[ANY, ANY, VM, VM] + [ANY] * 4,
-        out_specs=(ANY, ANY),
+        out_shape=(S((16, FK, 16, 128), f32), S((DEV, ROWS, 128), f32), S((DEV * ROWS, 128), f32)),
+        in_specs=[ANY, ANY] + [VM] * 8 + [ANY] * 4,
+        out_specs=(ANY,) * 3,
         scratch_shapes=[
-            V((2, FK, 144, 128), f32), V((16, FK, 16, 128), f32), V((K, 8, 128), f32), V((DEV, ROWS, 128), f32),
+            V((2, FK, 144, 128), f32), V((16, FK, 16, 128), f32), V((K, 8, 128), f32), V((DEV * ROWS, 128), f32),
+            V((128, 128), f32), V((256, 256), bf16), V((128, 128), i32), V((4 * 128, 128), f32),
+            V((NLON, NLAT // 2, ROWS, 128), f32), V((NLAT, NLON // 2, ROWS, 128), f32),
             V((FK, CI), f32), V((FK, CI), f32), V((CJ, 128), f32), V((CJ, 128), f32),
-            pltpu.SemaphoreType.DMA((4, 2)), pltpu.SemaphoreType.DMA((6,)),
+            pltpu.SemaphoreType.DMA((4, 2)), pltpu.SemaphoreType.DMA((15,)),
             pltpu.SemaphoreType.DMA((5,)), pltpu.SemaphoreType.DMA((4,)),
         ],
         compiler_params=pltpu.CompilerParams(vmem_limit_bytes=LIMIT, collective_id=0, has_side_effects=True),
         name="exchange_stencil",
-    )(st, out3, canopy_type, drag_table, rowlo, rowhi, colw, cole)
+    )(st, tuv, ilist, wlist, area, itemp, icond, ivel, canopy_type, drag_table, rowlo, rowhi, colw, cole)
     y, itemp_next = pl.pallas_call(
         finish_kernel,
         out_shape=(S((FK, CJ, CI), f32), S((64, 128), f32)),
@@ -588,7 +645,7 @@
         scratch_shapes=[
             V((16, FK, 16, 128), f32), V((16, FK, 16, 128), f32), V((2, CJ, 128), f32), V((K, 8, 128), f32),
             V((128, 128), i32), V((128, 128), i32), V((4 * 128, 128), f32), V((128, 128), f32),
-            V((4 * CJ, CI), f32), V((128, 128), f32), V((4 * CJ, 1024), bf16), V((CI, 512), bf16),
+            V((8 * CJ, CI), f32), V((128, 128), f32), V((2, 8 * CJ, 512), bf16), V((2, CI, 512), bf16),
             V((128, 512), bf16), V((128, 512), bf16),
             pltpu.SMEM((128, 128), i32), pltpu.SMEM((128, 128), i32), pltpu.SemaphoreType.DMA((7,)),
         ],

time: 62 us -> 54.7 us (0.88)
  the two profiles are of different devices: /device:TPU:33 before, /device:TPU:1 now
where the time goes in v3:
time: 54.7 us; the launch traced here: 54.5 us
  Pallas kernels  53.8 us (98%)
  between operations  0.64 us (1%)
    pallas_call x1, Pallas kernels, shards(): pl.pallas_call(stencil_kernel, out_shape=(S((16, FK, 16, 128), f32), S((D...  27.2 us
    pallas_call x1, Pallas kernels, shards(): pl.pallas_call(finish_kernel, out_shape=(S((FK, CJ, CI), f32), S((64, 128...  16.8 us
    pallas_call x1, Pallas kernels, shards(): pl.pallas_call(gather_kernel, out_shape=(S((3 * 128, 128), f32), S((FK, C...  9.82 us

profile of v3, /device:TPU:1, one launch (start us, length us, event | category | flops | bytes accessed | tf_op | source)
XLA Modules:
  0.0 54.5 jit_solution(4506293937323410479)
XLA Ops:
  0.6 9.8 %gather_slots.1 = (f32[384,128]{1,0:T(8,128)}, f32[80,256]{1,0:T(8,128)}, f32[80,256]{1,0:T(8,128)}, f32[128,128]{1,0:T(8,128)}, f32[128,128]{1,0:T(8,128)}) custom-call(f32[80,128,256]{2,1,0:T(8,128)} %bitcast.15, s32[128,128]{1,0:T(8,128)} %bitcast.18, s32[128,128]{1,0:T(8,128)} %bitcast.19), custom_call_target="tpu_custom_call" | custom-call | tf_op jit(solution)/shard_map/gather_slots/pallas_call | solution.py:610
  10.5 27.2 %exchange_stencil.1 = (f32[16,80,16,128]{3,2,1,0:T(8,128)}, f32[128,8,128]{2,1,0:T(8,128)}, f32[1024,128]{1,0:T(8,128)}) custom-call(f32[80,128,256]{2,1,0:T(8,128)} %bitcast.16, f32[384,128]{1,0:T(8,128)} %get-tuple-element.12.tuv, s32[128,128]{1,0:T(8,128)} %bitcast.22, s32[128,128]{1,0:T(8,128)} %bitcast.28, f32[1,64]{1,0:T(1,128)} %bitcast.31, ...), custom_call_target="tpu_custom_call" | custom-call | tf_op jit(solution)/shard_map/exchange_stencil/pallas_call | solution.py:624
  37.7 16.8 %scatter_solve.1 = (f32[80,128,256]{2,1,0:T(8,128)}, f32[64,128]{1,0:T(8,128)}) custom-call(f32[80,128,256]{2,1,0:T(8,128)} %bitcast.17, s32[128,128]{1,0:T(8,128)} %bitcast.20, s32[128,128]{1,0:T(8,128)} %bitcast.23, f32[16,80,16,128]{3,2,1,0:T(8,128)} %get-tuple-element.17.q_any, f32[1024,128]{1,0:T(8,128)} %bitcast.25, ...), custom_call_target="tpu_custom_call" | custom-call | tf_op jit(solution)/shard_map/scatter_solve/pallas_call | solution.py:640

commit v4 on v3

--- a/solution.py
+++ b/solution.py
@@ -32,7 +32,6 @@
 for _k in range(1, K):
     TOP.append(FWD[_k] * TOP[-1])
 
-VM = pl.BlockSpec(memory_space=pltpu.VMEM)
 ANY = pl.BlockSpec(memory_space=pl.ANY)
 LIMIT = 60 << 20
 
@@ -106,7 +105,7 @@
 
 
 def gather_kernel(
-    st, olist_any, olist,
+    loads, stores, st, olist_any, olist,
     tuv, rowlo, rowhi, colw, cole,
     full, surf, otab, opack, ogot, oflag, sems,
 ):
@@ -119,11 +118,14 @@
     state = [
         pltpu.make_async_copy(st.at[:, :, c * 128 : (c + 1) * 128], full.at[c], sems.at[2 + c]) for c in range(2)
     ]
-    for copy in tops + [flags] + state:
+    for copy in tops:
         copy.start()
+    loads[0].wait()
     pack_list(olist, opack)
     ogot[...] = jnp.zeros_like(ogot)
     pltpu.make_async_copy(surf, surf, sems.at[1]).wait()
+    for copy in [flags] + state:
+        copy.start()
     for n in range(3):
         for c in range(2):
             high, low = split(surf[n, c])
@@ -158,6 +160,12 @@
         for j in range(4):
             columns(4 * (t - 4) + j)
 
+    for fk in range(FK):
+        for c in range(2):
+            rowlo[fk : fk + 1, c * 128 : (c + 1) * 128] = full[c, fk, 0:1, :]
+            rowhi[fk : fk + 1, c * 128 : (c + 1) * 128] = full[c, fk, 127:128, :]
+    for copy in stores[1:]:
+        copy.start()
     flags.wait()
 
     @pl.loop(0, 32)
@@ -171,10 +179,7 @@
             even, odd = unpack(ogot, n, g)
             tuv[pl.ds(128 * n + 16 * g, 8, stride=2), :] = even
             tuv[pl.ds(128 * n + 16 * g + 1, 8, stride=2), :] = odd
-    for fk in range(FK):
-        for c in range(2):
-            rowlo[fk : fk + 1, c * 128 : (c + 1) * 128] = full[c, fk, 0:1, :]
-            rowhi[fk : fk + 1, c * 128 : (c + 1) * 128] = full[c, fk, 127:128, :]
+    stores[0].start()
 
 
 def stencil_row(m, buf, q, canopy, east_col, west_col, drag, lat):
@@ -234,9 +239,9 @@
 
 
 def ice_messages(ilist, wlist, area, itemp, icond, ivel, msg, itab, ipack, igot):
-    @pl.loop(0, 64, step=4)
+    @pl.loop(0, 64, step=8)
     def _(t):
-        for j in range(4):
+        for j in range(8):
             gather(t + j, ipack, itab, 4, 32, igot)
 
     areas = jnp.broadcast_to(jnp.concatenate([area[...], area[...]], axis=1), (8, 128))
@@ -254,7 +259,7 @@
 
 
 def stencil_kernel(
-    st, tuv, ilist, wlist, area, itemp, icond, ivel, canopy, table, rowlo, rowhi, colw, cole,
+    operands, _, st, tuv, ilist, wlist, area, itemp, icond, ivel, canopy, table, rowlo, rowhi, colw, cole,
     q_any, inb, out,
     buf, q, drag, msg, temps, itab, ipack, igot, mid_a, mid_b, north, south, east_col, west_col, sems, hops, halo_send, halo_recv,
 ):
@@ -270,10 +275,6 @@
         ]
         for g in range(4)
     ]
-    for pair in loads:
-        for copy in pair:
-            copy.start()
-
     surface = pltpu.make_async_copy(tuv.at[0:128], temps, hops.at[13])
     surface.start()
     barrier = pltpu.get_barrier_semaphore()
@@ -281,6 +282,11 @@
         pl.semaphore_signal(barrier, inc=1, device_id=(lax.rem(lon + i, NLON), lat), device_id_type=MESH)
     for i in range(1, NLAT):
         pl.semaphore_signal(barrier, inc=1, device_id=(lon, lax.rem(lat + i, NLAT)), device_id_type=MESH)
+    for copy in operands:
+        copy.wait()
+    for pair in loads:
+        for copy in pair:
+            copy.start()
     pack_list(ilist, ipack)
     for f in range(4):
         for c in range(2):
@@ -462,7 +468,7 @@
 
 
 def finish_kernel(
-    st, olist_any, ilist_any, q_any, inb, out, tuv, olist, ilist, canopy, table, itemp,
+    loads, stores, st, olist_any, ilist_any, q_any, inb, out, tuv, olist, ilist, canopy, table, itemp,
     y, itemp_next,
     q, ybuf, salt, drag, opack, ipack, oval, ival, oacc, iacc, owide, ocols, iwide, icols, oflag, iflag, sems,
 ):
@@ -475,11 +481,17 @@
         for c in range(2)
     ]
     state = pltpu.make_async_copy(q_any, q, sems.at[6])
+    oacc[...] = jnp.zeros_like(oacc)
+    iacc[...] = jnp.zeros_like(iacc)
+    for copy in loads[3:5]:
+        copy.wait()
+    pack_list(olist, opack)
+    pack_list(ilist, ipack)
+    for copy in loads[0:3] + loads[5:]:
+        copy.wait()
     for copy in flags + salts + [state]:
         copy.start()
     drag_levels(table, drag)
-    pack_list(olist, opack)
-    pack_list(ilist, ipack)
     for g in range(8):
         sides, ices = [], []
         for odd in range(2):
@@ -499,8 +511,6 @@
         first, second = pack(*ices)
         ival[8 * g : 8 * g + 8, :] = first
         ival[64 + 8 * g : 72 + 8 * g, :] = second
-    oacc[...] = jnp.zeros_like(oacc)
-    iacc[...] = jnp.zeros_like(iacc)
 
     def hot_columns(tile, packed, width, cols):
         for h in range(4):
@@ -554,6 +564,7 @@
             scatter_ice(16 + t)
 
     itemp_next[...] = itemp[...] - 0.25 * (iacc[0:64, :] + iacc[64:128, :])
+    stores[0].start()
     for copy in salts + [state]:
         copy.wait()
 
@@ -597,6 +608,40 @@
         pltpu.make_async_copy(part, part, sems.at[4 + c]).wait()
 
 
+def staged(kernel, args, moved, outs, kept, scratch, **options):
+    count, given = len(args), len(outs)
+
+    def body(*refs):
+        ins, results, rest = list(refs[:count]), list(refs[count : count + given]), list(refs[count + given :])
+        sems = rest.pop()
+        loads, stores = [], []
+        for i in moved:
+            place = rest.pop(0)
+            loads.append(pltpu.make_async_copy(ins[i], place, sems.at[len(loads)]))
+            ins[i] = place
+        for i in range(given):
+            if i not in kept:
+                place = rest.pop(0)
+                stores.append(pltpu.make_async_copy(place, results[i], sems.at[len(loads) + len(stores)]))
+                results[i] = place
+        for copy in loads:
+            copy.start()
+        kernel(loads, stores, *ins, *results, *rest)
+        for copy in stores:
+            copy.wait()
+
+    places = [pltpu.VMEM(args[i].shape, args[i].dtype) for i in moved]
+    places += [pltpu.VMEM(o.shape, o.dtype) for i, o in enumerate(outs) if i not in kept]
+    return pl.pallas_call(
+        body,
+        out_shape=outs,
+        in_specs=[ANY] * count,
+        out_specs=(ANY,) * given,
+        scratch_shapes=places + scratch + [pltpu.SemaphoreType.DMA((len(places),))],
+        **options,
+    )(*args)
+
+
 def shards(
     ocean_state, canopy_type, drag_table, ocean_list, ice_list, weight_list, area_table, ice_temp, ice_cond, ice_vel
 ):
@@ -607,26 +652,26 @@
     area = area_table.reshape(1, 64)
     S = jax.ShapeDtypeStruct
     V = pltpu.VMEM
-    tuv, rowlo, rowhi, colw, cole = pl.pallas_call(
+    tuv, rowlo, rowhi, colw, cole = staged(
         gather_kernel,
-        out_shape=(
-            S((3 * 128, 128), f32), S((FK, CI), f32), S((FK, CI), f32), S((CJ, 128), f32), S((CJ, 128), f32),
-        ),
-        in_specs=[ANY] * 2 + [VM],
-        out_specs=(VM,) * 5,
-        scratch_shapes=[
+        (st, olist, olist),
+        (2,),
+        (S((3 * 128, 128), f32), S((FK, CI), f32), S((FK, CI), f32), S((CJ, 128), f32), S((CJ, 128), f32)),
+        (),
+        [
             V((2, FK, CJ, 128), f32), V((3, 2, CJ, 128), f32), V((768, 256), bf16), V((128, 128), i32),
             V((3 * 128, 128), f32), pltpu.SMEM((128, 128), i32), pltpu.SemaphoreType.DMA((4,)),
         ],
         compiler_params=pltpu.CompilerParams(vmem_limit_bytes=LIMIT),
         name="gather_slots",
-    )(st, olist, olist)
-    q, inb, out = pl.pallas_call(
+    )
+    q, inb, out = staged(
         stencil_kernel,
-        out_shape=(S((16, FK, 16, 128), f32), S((DEV, ROWS, 128), f32), S((DEV * ROWS, 128), f32)),
-        in_specs=[ANY, ANY] + [VM] * 8 + [ANY] * 4,
-        out_specs=(ANY,) * 3,
-        scratch_shapes=[
+        (st, tuv, ilist, wlist, area, itemp, icond, ivel, canopy_type, drag_table, rowlo, rowhi, colw, cole),
+        range(2, 10),
+        (S((16, FK, 16, 128), f32), S((DEV, ROWS, 128), f32), S((DEV * ROWS, 128), f32)),
+        range(3),
+        [
             V((2, FK, 144, 128), f32), V((16, FK, 16, 128), f32), V((K, 8, 128), f32), V((DEV * ROWS, 128), f32),
             V((128, 128), f32), V((256, 256), bf16), V((128, 128), i32), V((4 * 128, 128), f32),
             V((NLON, NLAT // 2, ROWS, 128), f32), V((NLAT, NLON // 2, ROWS, 128), f32),
@@ -636,13 +681,14 @@
         ],
         compiler_params=pltpu.CompilerParams(vmem_limit_bytes=LIMIT, collective_id=0, has_side_effects=True),
         name="exchange_stencil",
-    )(st, tuv, ilist, wlist, area, itemp, icond, ivel, canopy_type, drag_table, rowlo, rowhi, colw, cole)
-    y, itemp_next = pl.pallas_call(
+    )
+    y, itemp_next = staged(
         finish_kernel,
-        out_shape=(S((FK, CJ, CI), f32), S((64, 128), f32)),
-        in_specs=[ANY] * 4 + [VM] * 8,
-        out_specs=(ANY, VM),
-        scratch_shapes=[
+        (st, olist, ilist, q, inb.reshape(DEV * ROWS, 128), out, tuv, olist, ilist, canopy_type, drag_table, itemp),
+        range(4, 12),
+        (S((FK, CJ, CI), f32), S((64, 128), f32)),
+        (0,),
+        [
             V((16, FK, 16, 128), f32), V((16, FK, 16, 128), f32), V((2, CJ, 128), f32), V((K, 8, 128), f32),
             V((128, 128), i32), V((128, 128), i32), V((4 * 128, 128), f32), V((128, 128), f32),
             V((8 * CJ, CI), f32), V((128, 128), f32), V((2, 8 * CJ, 512), bf16), V((2, CI, 512), bf16),
@@ -651,7 +697,7 @@
         ],
         compiler_params=pltpu.CompilerParams(vmem_limit_bytes=LIMIT),
         name="scatter_solve",
-    )(st, olist, ilist, q, inb.reshape(DEV * ROWS, 128), out, tuv, olist, ilist, canopy_type, drag_table, itemp)
+    )
     return y.reshape(ocean_state.shape), itemp_next.reshape(ice_temp.shape)
 
 

time: 54.7 us -> 52.4 us (0.958)
  Pallas kernels: 53.8 us -> 51.5 us
    pallas_call x3, Pallas kernels: 53.8 us -> 51.5 us  [staged(): pl.pallas_call(body, out_shape=outs, in_specs=[ANY] * count, out_specs=(A...]
where the time goes in v4:
time: 52.4 us; the launch traced here: 52.1 us
  Pallas kernels  51.5 us (98%)
  between operations  0.64 us (1%)
    pallas_call x3, Pallas kernels, staged(): pl.pallas_call(body, out_shape=outs, in_specs=[ANY] * count, out_specs=(A...  51.5 us

profile of v4, /device:TPU:1, one launch (start us, length us, event | category | flops | bytes accessed | tf_op | source)
XLA Modules:
  0.0 52.1 jit_solution(11226220221420010326)
XLA Ops:
  0.6 10.0 %gather_slots.1 = (f32[384,128]{1,0:T(8,128)}, f32[80,256]{1,0:T(8,128)}, f32[80,256]{1,0:T(8,128)}, f32[128,128]{1,0:T(8,128)}, f32[128,128]{1,0:T(8,128)}) custom-call(f32[80,128,256]{2,1,0:T(8,128)} %bitcast.15, s32[128,128]{1,0:T(8,128)} %bitcast.18, s32[128,128]{1,0:T(8,128)} %bitcast.19), custom_call_target="tpu_custom_call" | custom-call | tf_op jit(solution)/shard_map/gather_slots/pallas_call | solution.py:635
  10.6 25.3 %exchange_stencil.1 = (f32[16,80,16,128]{3,2,1,0:T(8,128)}, f32[128,8,128]{2,1,0:T(8,128)}, f32[1024,128]{1,0:T(8,128)}) custom-call(f32[80,128,256]{2,1,0:T(8,128)} %bitcast.16, f32[384,128]{1,0:T(8,128)} %get-tuple-element.12.refs_1_.refs_6_, s32[128,128]{1,0:T(8,128)} %bitcast.22, s32[128,128]{1,0:T(8,128)} %bitcast.28, f32[1,64]{1,0:T(1,128)} %bitcast.31, ...), custom_call_target="tpu_custom_call" | custom-call | tf_op jit(solution)/shard_map/exchange_stencil/pallas_call | solution.py:635
  35.9 16.2 %scatter_solve.1 = (f32[80,128,256]{2,1,0:T(8,128)}, f32[64,128]{1,0:T(8,128)}) custom-call(f32[80,128,256]{2,1,0:T(8,128)} %bitcast.17, s32[128,128]{1,0:T(8,128)} %bitcast.20, s32[128,128]{1,0:T(8,128)} %bitcast.23, f32[16,80,16,128]{3,2,1,0:T(8,128)} %get-tuple-element.17.refs_3_, f32[1024,128]{1,0:T(8,128)} %bitcast.25, ...), custom_call_target="tpu_custom_call" | custom-call | tf_op jit(solution)/shard_map/scatter_solve/pallas_call | solution.py:635

commit v5 on v4

--- a/solution.py
+++ b/solution.py
@@ -430,11 +430,10 @@
                     peer = lax.rem(lon + i, NLON)
                     hop(*second_b(peer), 6, (peer, lat)).start()
 
-        @pl.loop(0, 2)
-        def _(j):
-            m = 2 * g + j
-            stencil_row(m, buf, q, canopy, east_col, west_col, drag, lat)
-            pltpu.make_async_copy(q.at[m], q_any.at[m], hops.at[14]).start()
+        for j in range(2):
+            stencil_row(2 * g + j, buf, q, canopy, east_col, west_col, drag, lat)
+        for j in range(2):
+            pltpu.make_async_copy(q.at[2 * g + j], q_any.at[2 * g + j], hops.at[14]).start()
 
     pltpu.make_async_copy(q, q_any, hops.at[14]).wait()
     keep.wait()
@@ -532,23 +531,22 @@
                     owide[p, 512 * n + CJ * f : 512 * n + CJ * (f + 1), 128 * h : 128 * h + 128] = part
         add(owide[p], ocols[p], oacc)
 
-    def scatter_ice(tile):
-        hot_columns(tile, ipack, 128, icols)
+    def scatter_ice(tile, p=0):
+        hot_columns(tile, ipack, 128, icols.at[p])
         for h in range(4):
             mask = one_hot(ipack[pl.ds(4 * tile + h, 1), :] >> 7, 64)
             value = ival[pl.ds(4 * tile + h, 1), :]
             high = value.astype(bf16).astype(f32)
             for n, part in enumerate((high, value - high)):
                 part = jnp.where(mask, jnp.broadcast_to(part, (64, 128)), 0.0).astype(bf16)
-                iwide[64 * n : 64 * n + 64, 128 * h : 128 * h + 128] = part
-        add(iwide[...], icols[...], iacc)
-
-    @pl.loop(0, 16, step=2)
+                iwide[p, 64 * n : 64 * n + 64, 128 * h : 128 * h + 128] = part
+        add(iwide[p], icols[p], iacc)
+
+    @pl.loop(0, 16, step=4)
     def _(t):
-        scatter_ocean(t)
-        scatter_ocean(t + 1, 1)
-        scatter_ice(t)
-        scatter_ice(t + 1)
+        for j in range(4):
+            scatter_ocean(t + j, j)
+            scatter_ice(t + j, j)
 
     for copy in flags:
         copy.wait()
@@ -559,9 +557,13 @@
         def _():
             scatter_ocean(16 + t)
 
-        @pl.when(long_pairs(iflag, 8 * t, 8))
+
+    @pl.loop(0, 16, step=4)
+    def _(t):
+        @pl.when(long_pairs(iflag, 8 * t, 32))
         def _():
-            scatter_ice(16 + t)
+            for j in range(4):
+                scatter_ice(16 + t + j, j)
 
     itemp_next[...] = itemp[...] - 0.25 * (iacc[0:64, :] + iacc[64:128, :])
     stores[0].start()
@@ -691,8 +693,8 @@
         [
             V((16, FK, 16, 128), f32), V((16, FK, 16, 128), f32), V((2, CJ, 128), f32), V((K, 8, 128), f32),
             V((128, 128), i32), V((128, 128), i32), V((4 * 128, 128), f32), V((128, 128), f32),
-            V((8 * CJ, CI), f32), V((128, 128), f32), V((2, 8 * CJ, 512), bf16), V((2, CI, 512), bf16),
-            V((128, 512), bf16), V((128, 512), bf16),
+            V((8 * CJ, CI), f32), V((128, 128), f32), V((4, 8 * CJ, 512), bf16), V((4, CI, 512), bf16),
+            V((4, 128, 512), bf16), V((4, 128, 512), bf16),
             pltpu.SMEM((128, 128), i32), pltpu.SMEM((128, 128), i32), pltpu.SemaphoreType.DMA((7,)),
         ],
         compiler_params=pltpu.CompilerParams(vmem_limit_bytes=LIMIT),

time: 52.4 us -> 50.9 us (0.971)
  Pallas kernels: 51.5 us -> 50 us
    pallas_call x3, Pallas kernels: 51.5 us -> 50 us  [staged(): pl.pallas_call(body, out_shape=outs, in_specs=[ANY] * count, out_specs=(A...]
where the time goes in v5:
time: 50.9 us; the launch traced here: 50.7 us
  Pallas kernels  50 us (98%)
  between operations  0.64 us (1%)
    pallas_call x3, Pallas kernels, staged(): pl.pallas_call(body, out_shape=outs, in_specs=[ANY] * count, out_specs=(A...  50 us

profile of v5, /device:TPU:1, one launch (start us, length us, event | category | flops | bytes accessed | tf_op | source)
XLA Modules:
  0.0 50.7 jit_solution(15347966844672340170)
XLA Ops:
  0.6 10.0 %gather_slots.1 = (f32[384,128]{1,0:T(8,128)}, f32[80,256]{1,0:T(8,128)}, f32[80,256]{1,0:T(8,128)}, f32[128,128]{1,0:T(8,128)}, f32[128,128]{1,0:T(8,128)}) custom-call(f32[80,128,256]{2,1,0:T(8,128)} %bitcast.15, s32[128,128]{1,0:T(8,128)} %bitcast.18, s32[128,128]{1,0:T(8,128)} %bitcast.19), custom_call_target="tpu_custom_call" | custom-call | tf_op jit(solution)/shard_map/gather_slots/pallas_call | solution.py:637
  10.6 25.0 %exchange_stencil.1 = (f32[16,80,16,128]{3,2,1,0:T(8,128)}, f32[128,8,128]{2,1,0:T(8,128)}, f32[1024,128]{1,0:T(8,128)}) custom-call(f32[80,128,256]{2,1,0:T(8,128)} %bitcast.16, f32[384,128]{1,0:T(8,128)} %get-tuple-element.12.refs_1_.refs_6_, s32[128,128]{1,0:T(8,128)} %bitcast.22, s32[128,128]{1,0:T(8,128)} %bitcast.28, f32[1,64]{1,0:T(1,128)} %bitcast.31, ...), custom_call_target="tpu_custom_call" | custom-call | tf_op jit(solution)/shard_map/exchange_stencil/pallas_call | solution.py:637
  35.6 15.1 %scatter_solve.1 = (f32[80,128,256]{2,1,0:T(8,128)}, f32[64,128]{1,0:T(8,128)}) custom-call(f32[80,128,256]{2,1,0:T(8,128)} %bitcast.17, s32[128,128]{1,0:T(8,128)} %bitcast.20, s32[128,128]{1,0:T(8,128)} %bitcast.23, f32[16,80,16,128]{3,2,1,0:T(8,128)} %get-tuple-element.17.refs_3_, f32[1024,128]{1,0:T(8,128)} %bitcast.25, ...), custom_call_target="tpu_custom_call" | custom-call | tf_op jit(solution)/shard_map/scatter_solve/pallas_call | solution.py:637

commit v6 on v5

--- a/solution.py
+++ b/solution.py
@@ -403,7 +403,7 @@
                     st.at[:, 0:32, 0:128], buf.at[c, :, 8:40, :], sems.at[g // 2 + 1, c]
                 ).wait()
 
-        @pl.when(g == 3)
+        @pl.when(g == 2)
         def _():
             taken((NLON - 1) * NLAT // 2, 1)
             taken((NLAT - 1) * NLON // 2, 3)

time: 50.9 us -> 52 us (1.022)
  Pallas kernels: 50 us -> 51.2 us
    pallas_call x3, Pallas kernels: 50 us -> 51.2 us  [staged(): pl.pallas_call(body, out_shape=outs, in_specs=[ANY] * count, out_specs=(A...]
where the time goes in v6:
time: 52 us; the launch traced here: 51.8 us
  Pallas kernels  51.2 us (98%)
  between operations  0.64 us (1%)
    pallas_call x3, Pallas kernels, staged(): pl.pallas_call(body, out_shape=outs, in_specs=[ANY] * count, out_specs=(A...  51.2 us

profile of v6, /device:TPU:1, one launch (start us, length us, event | category | flops | bytes accessed | tf_op | source)
XLA Modules:
  0.0 51.8 jit_solution(1711890954510014014)
XLA Ops:
  0.6 10.0 %gather_slots.1 = (f32[384,128]{1,0:T(8,128)}, f32[80,256]{1,0:T(8,128)}, f32[80,256]{1,0:T(8,128)}, f32[128,128]{1,0:T(8,128)}, f32[128,128]{1,0:T(8,128)}) custom-call(f32[80,128,256]{2,1,0:T(8,128)} %bitcast.15, s32[128,128]{1,0:T(8,128)} %bitcast.18, s32[128,128]{1,0:T(8,128)} %bitcast.19), custom_call_target="tpu_custom_call" | custom-call | tf_op jit(solution)/shard_map/gather_slots/pallas_call | solution.py:637
  10.6 26.1 %exchange_stencil.1 = (f32[16,80,16,128]{3,2,1,0:T(8,128)}, f32[128,8,128]{2,1,0:T(8,128)}, f32[1024,128]{1,0:T(8,128)}) custom-call(f32[80,128,256]{2,1,0:T(8,128)} %bitcast.16, f32[384,128]{1,0:T(8,128)} %get-tuple-element.12.refs_1_.refs_6_, s32[128,128]{1,0:T(8,128)} %bitcast.22, s32[128,128]{1,0:T(8,128)} %bitcast.28, f32[1,64]{1,0:T(1,128)} %bitcast.31, ...), custom_call_target="tpu_custom_call" | custom-call | tf_op jit(solution)/shard_map/exchange_stencil/pallas_call | solution.py:637
  36.7 15.1 %scatter_solve.1 = (f32[80,128,256]{2,1,0:T(8,128)}, f32[64,128]{1,0:T(8,128)}) custom-call(f32[80,128,256]{2,1,0:T(8,128)} %bitcast.17, s32[128,128]{1,0:T(8,128)} %bitcast.20, s32[128,128]{1,0:T(8,128)} %bitcast.23, f32[16,80,16,128]{3,2,1,0:T(8,128)} %get-tuple-element.17.refs_3_, f32[1024,128]{1,0:T(8,128)} %bitcast.25, ...), custom_call_target="tpu_custom_call" | custom-call | tf_op jit(solution)/shard_map/scatter_solve/pallas_call | solution.py:637

commit v7 on v6

--- a/solution.py
+++ b/solution.py
@@ -403,7 +403,7 @@
                     st.at[:, 0:32, 0:128], buf.at[c, :, 8:40, :], sems.at[g // 2 + 1, c]
                 ).wait()
 
-        @pl.when(g == 2)
+        @pl.when(g == 4)
         def _():
             taken((NLON - 1) * NLAT // 2, 1)
             taken((NLAT - 1) * NLON // 2, 3)

time: 52 us -> 49.8 us (0.958)
  Pallas kernels: 51.2 us -> 48.9 us
    pallas_call x3, Pallas kernels: 51.2 us -> 48.9 us  [staged(): pl.pallas_call(body, out_shape=outs, in_specs=[ANY] * count, out_specs=(A...]
where the time goes in v7:
time: 49.8 us; the launch traced here: 49.6 us
  Pallas kernels  48.9 us (98%)
  between operations  0.64 us (1%)
    pallas_call x3, Pallas kernels, staged(): pl.pallas_call(body, out_shape=outs, in_specs=[ANY] * count, out_specs=(A...  48.9 us

profile of v7, /device:TPU:1, one launch (start us, length us, event | category | flops | bytes accessed | tf_op | source)
XLA Modules:
  0.0 49.6 jit_solution(12224809120397998303)
XLA Ops:
  0.6 10.0 %gather_slots.1 = (f32[384,128]{1,0:T(8,128)}, f32[80,256]{1,0:T(8,128)}, f32[80,256]{1,0:T(8,128)}, f32[128,128]{1,0:T(8,128)}, f32[128,128]{1,0:T(8,128)}) custom-call(f32[80,128,256]{2,1,0:T(8,128)} %bitcast.15, s32[128,128]{1,0:T(8,128)} %bitcast.18, s32[128,128]{1,0:T(8,128)} %bitcast.19), custom_call_target="tpu_custom_call" | custom-call | tf_op jit(solution)/shard_map/gather_slots/pallas_call | solution.py:637
  10.6 23.9 %exchange_stencil.1 = (f32[16,80,16,128]{3,2,1,0:T(8,128)}, f32[128,8,128]{2,1,0:T(8,128)}, f32[1024,128]{1,0:T(8,128)}) custom-call(f32[80,128,256]{2,1,0:T(8,128)} %bitcast.16, f32[384,128]{1,0:T(8,128)} %get-tuple-element.12.refs_1_.refs_6_, s32[128,128]{1,0:T(8,128)} %bitcast.22, s32[128,128]{1,0:T(8,128)} %bitcast.28, f32[1,64]{1,0:T(1,128)} %bitcast.31, ...), custom_call_target="tpu_custom_call" | custom-call | tf_op jit(solution)/shard_map/exchange_stencil/pallas_call | solution.py:637
  34.5 15.1 %scatter_solve.1 = (f32[80,128,256]{2,1,0:T(8,128)}, f32[64,128]{1,0:T(8,128)}) custom-call(f32[80,128,256]{2,1,0:T(8,128)} %bitcast.17, s32[128,128]{1,0:T(8,128)} %bitcast.20, s32[128,128]{1,0:T(8,128)} %bitcast.23, f32[16,80,16,128]{3,2,1,0:T(8,128)} %get-tuple-element.17.refs_3_, f32[1024,128]{1,0:T(8,128)} %bitcast.25, ...), custom_call_target="tpu_custom_call" | custom-call | tf_op jit(solution)/shard_map/scatter_solve/pallas_call | solution.py:637
